TPU v7x, 512 devices: a whole 4x8x8 slice. The times are simulated.
512 devices in a mesh: wide: 64 (over x, y, core), narrow: 8 (over z).
Axes of the slice: x: 4, y: 8, z: 8, core: 2. Of those that a mesh axis runs over, the one named last changes fastest.
Arguments:
- amplitudes: bfloat16 [3, 3072, 3072], P(None, 'wide', 'narrow'), may hold values from -6 to 6
- crossed: bfloat16 [3, 3072, 3072], P(None, 'wide', 'narrow'), may hold values from -6 to 6
- coulomb: bfloat16 [3, 3072, 3072], P(None, 'wide', 'narrow'), may hold values from -0.109375 to 0.109375
- exchange_int: bfloat16 [3, 3072, 3072], P(None, 'wide', 'narrow'), may hold values from -0.109375 to 0.109375
- block_order: int32 [3], replicated, may hold values from 1 to 3072, 6912 in all
Outputs:
- residual: bfloat16 [3, 3072, 3072], P(None, 'wide', 'narrow')
Inputs may be any that keep to these rules, and one draw needn't show every extreme that they name: `block_order`: the entries sum to 6912 and the largest is exactly 3072.
All inputs are finite; a program needn't handle non-finite values.
Results may differ from a plain program's by a relative error of at most 0.017.
Values may be sent and summed in bfloat16 or wider, within the bound.
No kernel may reach another device: no remote copies, remote signals or barrier semaphores. Data moves between devices by JAX's collectives and lax.ppermute only.
A program may use at most 128 MiB of HBM per device.

v0:
```python
import math

import jax
import jax.numpy as jnp
from jax import lax
from jax.sharding import PartitionSpec as P


def spread_rows(operand, grid_side):
    blocks, rows_local, k_local = operand.shape
    row_group = rows_local // grid_side
    shaped = operand.reshape(blocks, grid_side, 1, row_group, k_local)
    shaped = jnp.broadcast_to(shaped, (blocks, grid_side, grid_side, row_group, k_local))
    return shaped.reshape(blocks, grid_side * grid_side, row_group, k_local)


def spread_cols(operand, grid_side):
    blocks, rows_local, k_local = operand.shape
    row_group = rows_local // grid_side
    shaped = operand.reshape(blocks, 1, grid_side, row_group, k_local)
    shaped = jnp.broadcast_to(shaped, (blocks, grid_side, grid_side, row_group, k_local))
    return shaped.reshape(blocks, grid_side * grid_side, row_group, k_local)


def tile_product(left_tile, right_tile):
    left_tile = left_tile.reshape(left_tile.shape[0], -1, left_tile.shape[-1])
    right_tile = right_tile.reshape(right_tile.shape[0], -1, right_tile.shape[-1])
    return jnp.einsum("hrk,hck->hrc", left_tile, right_tile, preferred_element_type=jnp.float32)


def both_products(pieces):
    return tile_product(pieces[0], pieces[1]) + tile_product(pieces[2], pieces[3])


def local(amplitudes, crossed, coulomb, exchange_int, block_order):
    wide_count = lax.axis_size("wide")
    grid_side = math.isqrt(wide_count)
    blocks, rows_local, k_local = amplitudes.shape
    row_group = rows_local // grid_side
    k_start = lax.axis_index("narrow") * k_local
    positions = k_start + jnp.arange(k_local, dtype=jnp.int32)
    live_cols = (positions[None, :] < block_order[:, None]).astype(jnp.bfloat16)
    masked_amp = amplitudes * live_cols[:, None, :]
    masked_cross = crossed * live_cols[:, None, :]
    partial_value = both_products(
        (
            lax.all_to_all(
                spread_rows(masked_amp, grid_side), "wide", split_axis=1, concat_axis=2, tiled=True
            ),
            lax.all_to_all(
                spread_cols(coulomb, grid_side), "wide", split_axis=1, concat_axis=2, tiled=True
            ),
            lax.all_to_all(
                spread_rows(masked_cross, grid_side),
                "wide",
                split_axis=1,
                concat_axis=2,
                tiled=True,
            ),
            lax.all_to_all(
                spread_cols(exchange_int, grid_side),
                "wide",
                split_axis=1,
                concat_axis=2,
                tiled=True,
            ),
        )
    )
    tile_size = partial_value.shape[1]
    outgoing = partial_value.astype(jnp.bfloat16).reshape(blocks, wide_count, row_group, tile_size)
    arrived = lax.all_to_all(outgoing, "wide", split_axis=1, concat_axis=1, tiled=True)
    arranged = arrived.reshape(blocks, grid_side, grid_side, row_group, wide_count, row_group)
    arranged = arranged.transpose(0, 1, 3, 4, 2, 5).reshape(
        blocks, rows_local, wide_count * rows_local
    )
    summed = lax.psum_scatter(
        arranged.astype(jnp.float32).astype(jnp.bfloat16), "narrow", scatter_dimension=2, tiled=True
    )
    row_positions = lax.axis_index("wide") * rows_local + jnp.arange(rows_local, dtype=jnp.int32)
    live_rows = (row_positions[None, :] < block_order[:, None]).astype(jnp.bfloat16)
    return summed * live_rows[:, :, None] * live_cols[:, None, :]


def solution(mesh):
    in_specs = (
        P(None, "wide", "narrow"),
        P(None, "wide", "narrow"),
        P(None, "wide", "narrow"),
        P(None, "wide", "narrow"),
        P(),
    )
    out_specs = P(None, "wide", "narrow")
    return jax.shard_map(local, mesh=mesh, in_specs=in_specs, out_specs=out_specs, check_vma=False)
```

profile of v0, /device:TPU:6, one launch (start us, length us, event | category | flops | bytes accessed | tf_op | source)
XLA Modules:
  0.0 364.2 jit_solution(8319079595166353040)
XLA Ops:
  6.5 0.7 compare_convert_fusion
  7.3 1.0 broadcast_multiply_fusion
  8.3 1.1 broadcast_in_dim.17
  9.5 0.0 copy-start.4
  9.5 10.9 %all-to-all-start = ((bf16[3,64,6,384]{3,2,0,1:T(8,128)(2,1)}), bf16[3,64,6,384]{3,2,0,1:T(8,128)(2,1)S(1)}, u32[]{:S(2)}, u32[]{:S(2)}) async-start(bf16[3,64,6,384]{3,2,0,1:T(8,128)(2,1)} %bitcast), calls=%async_computation | async-start | bytes 2359296 | tf_op jit(solution)/shard_map/all_to_all | solution.py:47
  20.4 0.0 copy-done.4
  20.5 29.1 %all-to-all-done = bf16[3,64,6,384]{3,2,0,1:T(8,128)(2,1)S(1)} async-done(((bf16[3,64,6,384]{3,2,0,1:T(8,128)(2,1)}), bf16[3,64,6,384]{3,2,0,1:T(8,128)(2,1)S(1)}, u32[]{:S(2)}, u32[]{:S(2)}) %all-to-all-start) | async-done | bytes 884768 | tf_op jit(solution)/shard_map/all_to_all | solution.py:47
  49.6 1.2 broadcast_in_dim.19
  50.8 8.3 %all-to-all-start.1 = ((bf16[3,64,6,384]{3,2,0,1:T(8,128)(2,1)}), bf16[3,64,6,384]{3,2,0,1:T(8,128)(2,1)S(1)}, u32[]{:S(2)}, u32[]{:S(2)}) async-start(bf16[3,64,6,384]{3,2,0,1:T(8,128)(2,1)} %bitcast.1), calls=%async_computation.1 | async-start | bytes 2359296 | tf_op jit(solution)/shard_map/all_to_all | solution.py:50
  59.2 29.1 %all-to-all-done.1 = bf16[3,64,6,384]{3,2,0,1:T(8,128)(2,1)S(1)} async-done(((bf16[3,64,6,384]{3,2,0,1:T(8,128)(2,1)}), bf16[3,64,6,384]{3,2,0,1:T(8,128)(2,1)S(1)}, u32[]{:S(2)}, u32[]{:S(2)}) %all-to-all-start.1) | async-done | bytes 884768 | tf_op jit(solution)/shard_map/all_to_all | solution.py:50
  88.4 1.1 broadcast_in_dim.41
  89.5 8.3 %all-to-all-start.2 = ((bf16[3,64,6,384]{3,2,0,1:T(8,128)(2,1)}), bf16[3,64,6,384]{3,2,0,1:T(8,128)(2,1)S(1)}, u32[]{:S(2)}, u32[]{:S(2)}) async-start(bf16[3,64,6,384]{3,2,0,1:T(8,128)(2,1)} %bitcast.22), calls=%async_computation.2 | async-start | bytes 2359296 | tf_op jit(solution)/shard_map/all_to_all | solution.py:53
  97.8 1.6 broadcast_in_dim.42
  99.4 1.6 copy.15
  101.0 26.0 %all-to-all-done.2 = bf16[3,64,6,384]{3,2,0,1:T(8,128)(2,1)S(1)} async-done(((bf16[3,64,6,384]{3,2,0,1:T(8,128)(2,1)}), bf16[3,64,6,384]{3,2,0,1:T(8,128)(2,1)S(1)}, u32[]{:S(2)}, u32[]{:S(2)}) %all-to-all-start.2) | async-done | bytes 884768 | tf_op jit(solution)/shard_map/all_to_all | solution.py:53
  127.1 2.1 broadcast_in_dim.43
  129.1 8.5 %all-to-all-start.3 = ((bf16[3,64,6,384]{3,2,0,1:T(8,128)(2,1)}), bf16[3,64,6,384]{3,2,0,1:T(8,128)(2,1)}, u32[]{:S(2)}, u32[]{:S(2)}) async-start(bf16[3,64,6,384]{3,2,0,1:T(8,128)(2,1)} %bitcast.21), calls=%async_computation.3 | async-start | bytes 2359296 | tf_op jit(solution)/shard_map/all_to_all | solution.py:60
  137.7 0.0 reduce-scatter.4.cloned.1.call-start
  137.7 1.1 copy.10
  138.9 2.2 reshape.117
  141.0 0.1 copy.12
  141.1 1.2 reshape.119
  142.3 0.1 copy.14
  142.5 1.2 reshape.121
  143.7 23.1 %all-to-all-done.3 = bf16[3,64,6,384]{3,2,0,1:T(8,128)(2,1)} async-done(((bf16[3,64,6,384]{3,2,0,1:T(8,128)(2,1)}), bf16[3,64,6,384]{3,2,0,1:T(8,128)(2,1)}, u32[]{:S(2)}, u32[]{:S(2)}) %all-to-all-start.3) | async-done | bytes 884768 | tf_op jit(solution)/shard_map/all_to_all | solution.py:60
  166.8 1.4 copy.16
  168.2 0.0 copy-start
  168.2 0.0 copy-start.1
  168.2 1.2 reshape.123
  169.4 0.0 copy-done
  169.4 0.5 copy-done.1
  170.0 0.0 copy-start.2
  170.0 0.0 copy-start.3
  170.0 0.7 fusion
  170.7 0.4 copy-done.2
  171.1 0.3 copy-done.3
  171.4 0.7 add_convert_fusion
  172.1 0.3 reshape.124
  172.4 0.1 copy.17
  172.6 37.3 %all_to_all.20 = bf16[3,64,6,384]{3,2,0,1:T(8,128)(2,1)S(1)} all-to-all(bf16[3,64,6,384]{3,2,0,1:T(8,128)(2,1)S(1)} %copy.17), channel_id=1, replica_groups=mesh['wide'=64,'narrow'=8] {'wide'}, dimensions={1} | all-to-all | bytes 1769472 | tf_op jit(solution)/shard_map/all_to_all | solution.py:71
  209.9 1.2 copy.18
  211.1 11.5 %reshape.125 = bf16[3,8,8,6,64,6]{2,1,5,4,3,0:T(8,128)(2,1)} reshape(bf16[3,64,6,384]{1,3,2,0:T(8,128)(2,1)S(1)} %copy.18) | data formatting | bytes 1769472 | tf_op jit(solution)/shard_map/reshape | solution.py:72
  222.6 60.0 %copy.22 = bf16[3,8,6,64,8,6]{2,1,0,5,4,3:T(8,128)(2,1)} copy(bf16[3,8,6,64,8,6]{4,1,5,3,2,0:T(8,128)(2,1)} %bitcast.19) | data formatting | bytes 1769472
  282.6 23.3 %reshape.129 = bf16[3,48,3072]{1,0,2:T(4,128)(2,1)S(1)} reshape(bf16[3,8,6,64,8,6]{2,1,0,5,4,3:T(8,128)(2,1)} %copy.22) | data formatting | bytes 1769472
  306.0 3.2 reshape.127
  309.2 0.0 copy-start.5
  309.2 0.0 reduce-scatter.4.cloned.1.call-update
  309.2 0.6 copy-done.5
  309.8 0.1 compare_convert_fusion.1
  309.9 45.4 %reduce-scatter.4.cloned.1.call-done = bf16[384,144]{1,0:T(8,128)(2,1)} async-done(((bf16[3072,144]{1,0:T(8,128)(2,1)}), bf16[384,144]{1,0:T(8,128)(2,1)}) %reduce-scatter.4.cloned.1.call-update) | async-done | bytes 110608
  355.3 1.1 reshape.128
  356.4 0.2 copy.21
  356.7 0.7 multiply_multiply_fusion
  (8 shorter events, 0.2 us)
Async XLA Ops:
  9.5 10.9 %copy-start.4 = (bf16[3,48,384]{2,1,0:T(8,128)(2,1)S(1)}, bf16[3,48,384]{2,1,0:T(8,128)(2,1)}, u32[]{:S(2)}) copy-start(bf16[3,48,384]{2,1,0:T(8,128)(2,1)} %param.7) | copy-start | bytes 331780
  9.5 40.2 %all-to-all-start = ((bf16[3,64,6,384]{3,2,0,1:T(8,128)(2,1)}), bf16[3,64,6,384]{3,2,0,1:T(8,128)(2,1)S(1)}, u32[]{:S(2)}, u32[]{:S(2)}) async-start(bf16[3,64,6,384]{3,2,0,1:T(8,128)(2,1)} %bitcast), calls=%async_computation | async-start | bytes 2359296 | tf_op jit(solution)/shard_map/all_to_all | solution.py:47
  50.8 37.6 %all-to-all-start.1 = ((bf16[3,64,6,384]{3,2,0,1:T(8,128)(2,1)}), bf16[3,64,6,384]{3,2,0,1:T(8,128)(2,1)S(1)}, u32[]{:S(2)}, u32[]{:S(2)}) async-start(bf16[3,64,6,384]{3,2,0,1:T(8,128)(2,1)} %bitcast.1), calls=%async_computation.1 | async-start | bytes 2359296 | tf_op jit(solution)/shard_map/all_to_all | solution.py:50
  89.5 37.6 %all-to-all-start.2 = ((bf16[3,64,6,384]{3,2,0,1:T(8,128)(2,1)}), bf16[3,64,6,384]{3,2,0,1:T(8,128)(2,1)S(1)}, u32[]{:S(2)}, u32[]{:S(2)}) async-start(bf16[3,64,6,384]{3,2,0,1:T(8,128)(2,1)} %bitcast.22), calls=%async_computation.2 | async-start | bytes 2359296 | tf_op jit(solution)/shard_map/all_to_all | solution.py:53
  129.1 37.7 %all-to-all-start.3 = ((bf16[3,64,6,384]{3,2,0,1:T(8,128)(2,1)}), bf16[3,64,6,384]{3,2,0,1:T(8,128)(2,1)}, u32[]{:S(2)}, u32[]{:S(2)}) async-start(bf16[3,64,6,384]{3,2,0,1:T(8,128)(2,1)} %bitcast.21), calls=%async_computation.3 | async-start | bytes 2359296 | tf_op jit(solution)/shard_map/all_to_all | solution.py:60
  137.7 217.7 %reduce-scatter.4.cloned.1.call-start = ((), (), s32[]{:S(2)}) async-start(), calls=%async_computation.6 | async-start | bytes 1769472
  168.2 1.2 copy-start
  168.2 1.7 copy-start.1
  170.0 1.2 copy-start.2
  170.0 1.4 copy-start.3
  309.2 0.7 copy-start.5
Sparse Core Ops, SparseCore 0:
  309.3 45.9 reduce-scatter.3
where the time goes:
time: 366 us; the launch traced here: 364 us
  waiting for transfers between devices  153 us (42%)
  local copies, waits for them, and re-layouts  120 us (33%)
  blocking collectives  37.3 us (10%)
  starting transfers between devices  36.1 us (10%)
  between operations  13.6 us (4%)
    unnamed x17, local copies, waits for them, and re-layouts  89.7 us
    unnamed x2, waiting for transfers between devices  45.4 us
    all_to_all x1, blocking collectives, local(): lax.all_to_all(outgoing, 'wide', split_axis=1, concat_axis=1, tiled=True)  37.3 us
    all_to_all x1, waiting for transfers between devices, local(): lax.all_to_all(spread_cols(coulomb, grid_side), 'wide', split_axis=1, con...  29.1 us
    all_to_all x1, waiting for transfers between devices, local(): lax.all_to_all(spread_rows(masked_amp, grid_side), 'wide', split_axis=1,...  29.1 us
    all_to_all x1, waiting for transfers between devices, local(): lax.all_to_all(spread_rows(masked_cross, grid_side), 'wide', split_axis=1...  26 us
    all_to_all x1, waiting for transfers between devices, local(): lax.all_to_all(spread_cols(exchange_int, grid_side), 'wide', split_axis=1...  23.1 us
    reshape x1, local copies, waits for them, and re-layouts, local(): arrived.reshape(blocks, grid_side, grid_side, row_group, wide_count, row_...  11.5 us
  transfers between devices with their start and end apart: 5, of which 5 were waited for; matrix products, arithmetic and copies ran while one was open for 3% of the time, Pallas kernels for 0%

commit v1 on v0

v1 whole, which is shorter than its diff:
```python
import jax
import jax.numpy as jnp
from jax import lax
from jax.experimental import pallas as pl
from jax.experimental.pallas import tpu as pltpu
from jax.sharding import Mesh, PartitionSpec as P

NX, NY, NC, NZ = 4, 8, 2, 8
NH, ROWS, DEPTH = 3, 48, 384


def tile_kernel(order_ref, left_ref, right_ref, out_ref, *, col_tile):
    x, y, c, z = (order_ref[NH + i] for i in range(4))
    col = lax.broadcasted_iota(jnp.int32, (1, DEPTH), 1)
    for h in range(NH):
        length = order_ref[h]
        live_k = (z * DEPTH + col) < length
        total = None
        for pair in range(2):
            left = left_ref[:, pair, h].reshape(NX * ROWS, DEPTH)
            left = jnp.where(live_k, left, jnp.zeros_like(left))
            right = right_ref[:, pair, h].reshape(NY * NC * ROWS, DEPTH)
            part = lax.dot_general(
                left, right, (((1,), (1,)), ((), ())), preferred_element_type=jnp.float32
            )
            total = part if total is None else total + part
        for xx in range(NX):
            row = lax.broadcasted_iota(jnp.int32, (ROWS, 1), 0)
            row = ((xx * NY + y) * NC + c) * ROWS + row
            for half in range(2):
                b = (x * 2 + half) * col_tile + col
                live = (row < length) & (b < length)
                block = total[xx * ROWS : (xx + 1) * ROWS, half * col_tile : (half + 1) * col_tile]
                out_ref[xx * 2 + half, h] = jnp.where(live, block, 0.0).astype(jnp.bfloat16)


def local(amplitudes, crossed, coulomb, exchange_int, block_order):
    x, y, c, z = (lax.axis_index(n) for n in ("x", "y", "c", "z"))
    place = jnp.concatenate([block_order, jnp.stack([x, y, c, z]).astype(jnp.int32)])
    left = lax.all_gather(jnp.stack([amplitudes, crossed]), "x")
    right = lax.all_gather(jnp.stack([coulomb, exchange_int]), ("y", "c"))
    col_tile = NY * NC * ROWS // 2
    pieces = pl.pallas_call(
        lambda *refs: tile_kernel(*refs, col_tile=col_tile),
        out_shape=jax.ShapeDtypeStruct((NX * 2, NH, ROWS, col_tile), jnp.bfloat16),
        in_specs=[
            pl.BlockSpec(memory_space=pltpu.SMEM),
            pl.BlockSpec(memory_space=pltpu.VMEM),
            pl.BlockSpec(memory_space=pltpu.VMEM),
        ],
        out_specs=pl.BlockSpec(memory_space=pltpu.VMEM),
        compiler_params=pltpu.CompilerParams(vmem_limit_bytes=32 * 2**20),
    )(place, left, right)
    summed = lax.psum_scatter(pieces, "z", scatter_dimension=0)
    moves = [
        (xs * NZ + xd * 2 + half, xd * NZ + xs * 2 + half)
        for xs in range(NX)
        for xd in range(NX)
        for half in range(2)
    ]
    return lax.ppermute(summed, ("x", "z"), moves)


def solution(mesh):
    grid = Mesh(mesh.devices.reshape(NX, NY, NC, NZ), ("x", "y", "c", "z"))
    spec = P(None, ("x", "y", "c"), "z")
    return jax.shard_map(
        local, mesh=grid, in_specs=(spec,) * 4 + (P(),), out_specs=spec, check_vma=False
    )
```

time: 366 us -> 124 us (0.34)
  local copies, waits for them, and re-layouts: 120 us -> 3.38 us
  waiting for transfers between devices: 153 us -> 80.4 us
  starting transfers between devices: 36.1 us -> 3.37 us
  blocking collectives: 37.3 us -> 16.1 us
    all_to_all x4 -> x0, waiting for transfers between devices: 107 us -> none  [the longest x1 29.1 us: local(): lax.all_to_all(spread_cols(coulomb, grid_side), 'wide', split_axis=1, con...]
    unnamed x17 -> x3, local copies, waits for them, and re-layouts: 89.7 us -> 2.65 us
    unnamed x2, waiting for transfers between devices: 45.4 us -> 0.03 us
    reduce_scatter x0 -> x1, waiting for transfers between devices: none -> 40.6 us  [local(): summed = lax.psum_scatter(pieces, 'z', scatter_dimension=0)]
    all_to_all x1 -> x0, blocking collectives: 37.3 us -> none  [local(): lax.all_to_all(outgoing, 'wide', split_axis=1, concat_axis=1, tiled=True)]
    all_to_all x4 -> x0, starting transfers between devices: 36.1 us -> none  [the longest x1 10.9 us: local(): lax.all_to_all(spread_rows(masked_amp, grid_side), 'wide', split_axis=1,...]
    all_gather x0 -> x1, waiting for transfers between devices: none -> 31.9 us  [local(): right = lax.all_gather(jnp.stack([coulomb, exchange_int]), ('y', 'c'))]
    reshape x7 -> x0, local copies, waits for them, and re-layouts: 17.7 us -> none  [the longest x1 11.5 us: local(): arrived.reshape(blocks, grid_side, grid_side, row_group, wide_count, row_...]
  transfers between devices with their start and end apart: 5 -> 3, of which waited for: 5 -> 3; matrix products, arithmetic and copies ran while one was open for 3% -> 1% of each run, Pallas kernels for 0% -> 0%
where the time goes in v1:
time: 124 us; the launch traced here: 122 us
  waiting for transfers between devices  80.4 us (65%)
  blocking collectives  16.1 us (13%)
  between operations  13.4 us (11%)
  local copies, waits for them, and re-layouts  3.38 us (3%)
  starting transfers between devices  3.37 us (3%)
  Pallas kernels  2.77 us (2%)
  other arithmetic  2.64 us (2%)
    reduce_scatter x1, waiting for transfers between devices, local(): summed = lax.psum_scatter(pieces, 'z', scatter_dimension=0)  40.6 us
    all_gather x1, waiting for transfers between devices, local(): right = lax.all_gather(jnp.stack([coulomb, exchange_int]), ('y', 'c'))  31.9 us
    all_gather x1, blocking collectives, local(): left = lax.all_gather(jnp.stack([amplitudes, crossed]), 'x')  16.1 us
    ppermute x1, waiting for transfers between devices, local(): return lax.ppermute(summed, ('x', 'z'), moves)  7.83 us
    ppermute x1, starting transfers between devices, local(): return lax.ppermute(summed, ('x', 'z'), moves)  3.33 us
    pallas_call x1, Pallas kernels, local(): pl.pallas_call(lambda *refs: tile_kernel(*refs, col_tile=col_tile), out_s...  2.77 us
    unnamed x3, local copies, waits for them, and re-layouts  2.65 us
  transfers between devices with their start and end apart: 3, of which 3 were waited for; matrix products, arithmetic and copies ran while one was open for 1% of the time, Pallas kernels for 0%

profile of v1, /device:TPU:6, one launch (start us, length us, event | category | flops | bytes accessed | tf_op | source)
XLA Modules:
  0.0 122.1 jit_solution(12530049997359967670)
XLA Ops:
  6.5 0.0 all-gather.4.cloned.1.call-start
  6.5 1.7 %pad_maximum_fusion.1 = bf16[2,3,48,384]{3,2,1,0:T(8,128)(2,1)} fusion(bf16[1,3,48,384]{3,2,1,0:T(8,128)(2,1)} %bitcast.13, bf16[1,3,48,384]{3,2,1,0:T(8,128)(2,1)} %bitcast.14), kind=kLoop, calls=%fused_computation.1 | loop fusion | flops 110592 | bytes 442368 | tf_op jit(solution)/shard_map/stack | solution.py:41
  8.2 0.0 all-gather.4.cloned.1.call-update
  8.2 0.0 reduce-scatter.2.cloned.1.call-start
  8.3 0.7 concatenate.3.refs_0_
  9.0 1.0 pad_maximum_fusion
  10.0 16.1 %all-gather = bf16[8,3,48,384]{3,2,1,0:T(8,128)(2,1)S(1)} all-gather(bf16[2,3,48,384]{3,2,1,0:T(8,128)(2,1)S(1)} %pad_maximum_fusion), channel_id=2, replica_groups=mesh['x'=4,'y'=8,'c'=2,'z'=8] {'x'}, dimensions={0}, use_global_device_ids=true | all-gather | bytes 1105920 | tf_op jit(solution)/shard_map/all_gather | solution.py:40
  26.1 31.9 %all-gather.4.cloned.1.call-done = bf16[32,3,48,384]{3,2,1,0:T(8,128)(2,1)} async-done(((bf16[2,3,48,384]{3,2,1,0:T(8,128)(2,1)}), bf16[32,3,48,384]{3,2,1,0:T(8,128)(2,1)}) %all-gather.4.cloned.1.call-update) | async-done | bytes 3538960 | tf_op jit(solution)/shard_map/all_gather | solution.py:41
  58.1 0.0 copy-start
  58.1 2.0 %copy-done = bf16[32,3,48,384]{3,2,1,0:T(8,128)(2,1)S(1)} copy-done((bf16[32,3,48,384]{3,2,1,0:T(8,128)(2,1)S(1)}, bf16[32,3,48,384]{3,2,1,0:T(8,128)(2,1)}, u32[]{:S(2)}) %copy-start) | copy-done | bytes 3538968
  60.1 2.8 %shard_map.55 = bf16[8,3,48,384]{3,2,1,0:T(8,128)(2,1)} custom-call(s32[7]{0:T(128)S(1)} %concatenate.3.refs_0_, bf16[4,2,3,48,384]{4,3,2,1,0:T(8,128)(2,1)S(1)} %bitcast.12, bf16[16,2,3,48,384]{4,3,2,1,0:T(8,128)(2,1)S(1)} %bitcast.11), custom_call_target="tpu_custom_call" | custom-call | tf_op jit(solution)/shard_map/pallas_call | solution.py:43
  62.9 0.0 reduce-scatter.2.cloned.1.call-update
  62.9 40.6 %reduce-scatter.2.cloned.1.call-done = bf16[1,3,48,384]{3,2,1,0:T(8,128)(2,1)} async-done(((bf16[8,3,48,384]{3,2,1,0:T(8,128)(2,1)}), bf16[1,3,48,384]{3,2,1,0:T(8,128)(2,1)}) %reduce-scatter.2.cloned.1.call-update) | async-done | bytes 110608 | tf_op jit(solution)/shard_map/reduce_scatter | solution.py:54
  103.5 3.3 %collective-permute-start = (bf16[3,48,384]{2,1,0:T(8,128)(2,1)}, bf16[3,48,384]{2,1,0:T(8,128)(2,1)S(1)}, u32[]{:S(2)}, u32[]{:S(2)}) collective-permute-start(bf16[3,48,384]{2,1,0:T(8,128)(2,1)} %bitcast.17), channel_id=1, source_target_pairs={{0,0},{1,1},{2,128},{3,129},{4,256},{5,257},{6,384},{7,385},{128,2... | collective-permute-start | bytes 331784 | tf_op jit(solution)/shard_map/ppermute | solution.py:61
  106.8 7.8 %collective-permute-done = bf16[3,48,384]{2,1,0:T(8,128)(2,1)S(1)} collective-permute-done((bf16[3,48,384]{2,1,0:T(8,128)(2,1)}, bf16[3,48,384]{2,1,0:T(8,128)(2,1)S(1)}, u32[]{:S(2)}, u32[]{:S(2)}) %collective-permute-start) | collective-permute-done | bytes 110624 | tf_op jit(solution)/shard_map/ppermute | solution.py:61
  114.7 0.6 copy.7
Async XLA Ops:
  6.5 51.5 %all-gather.4.cloned.1.call-start = ((), (), s32[]{:S(2)}) async-start(), calls=%async_computation.2 | async-start | bytes 3760128 | tf_op jit(solution)/shard_map/all_gather | solution.py:41
  8.2 95.3 %reduce-scatter.2.cloned.1.call-start = ((), (), s32[]{:S(2)}) async-start(), calls=%async_computation.1 | async-start | bytes 995328 | tf_op jit(solution)/shard_map/reduce_scatter | solution.py:54
  58.1 2.0 %copy-start = (bf16[32,3,48,384]{3,2,1,0:T(8,128)(2,1)S(1)}, bf16[32,3,48,384]{3,2,1,0:T(8,128)(2,1)}, u32[]{:S(2)}) copy-start(bf16[32,3,48,384]{3,2,1,0:T(8,128)(2,1)} %all-gather.4.cloned.1.call-done) | copy-start | bytes 10616836
  103.5 11.2 %collective-permute-start = (bf16[3,48,384]{2,1,0:T(8,128)(2,1)}, bf16[3,48,384]{2,1,0:T(8,128)(2,1)S(1)}, u32[]{:S(2)}, u32[]{:S(2)}) collective-permute-start(bf16[3,48,384]{2,1,0:T(8,128)(2,1)} %bitcast.17), channel_id=1, source_target_pairs={{0,0},{1,1},{2,128},{3,129},{4,256},{5,257},{6,384},{7,385},{128,2... | collective-permute-start | bytes 331784 | tf_op jit(solution)/shard_map/ppermute | solution.py:61
Sparse Core Ops, SparseCore 0:
  9.5 48.5 all-gather.3
  63.0 40.4 reduce-scatter.1

commit v2 on v1

v2 whole, which is shorter than its diff:
```python
import jax
import jax.numpy as jnp
from jax import lax
from jax.experimental import pallas as pl
from jax.experimental.pallas import tpu as pltpu
from jax.sharding import Mesh, PartitionSpec as P

NX, NY, NC, NZ = 4, 8, 2, 8
NH, ROWS, DEPTH = 3, 48, 384
HALF = NY // 2 * ROWS
BLOCK = (2, NH, ROWS, DEPTH)
PIECE = (NH, ROWS, DEPTH)
VMEM = pl.BlockSpec(memory_space=pltpu.VMEM)
SMEM = pl.BlockSpec(memory_space=pltpu.SMEM)
ANY = pl.BlockSpec(memory_space=pl.ANY)
PARAMS = pltpu.CompilerParams(vmem_limit_bytes=32 * 2**20)
BF16 = jnp.bfloat16


def left_kernel(place, amp, cross, _, out):
    k = place[NH + 3] * DEPTH + lax.broadcasted_iota(jnp.int32, (1, DEPTH), 1)
    for h in range(NH):
        live = k < place[h]
        for pair, ref in enumerate((amp, cross)):
            block = jnp.where(live, ref[h], jnp.zeros_like(ref[h]))
            for e in range(NX):
                out[e, pair, h] = block


def copy_kernel(src, _, out):
    out[...] = src[...]


def tile_kernel(place, own, other, *refs):
    rights, (out, lhs, rhs) = refs[:NY], refs[NY:]
    y, c = place[NH + 1], place[NH + 2]
    for x in range(NX):
        for h in range(NH):
            for pair in range(2):
                lhs[h, pair, 2 * x + c] = own[x, pair, h]
                lhs[h, pair, 2 * x + 1 - c] = other[x, pair, h]
    for d in range(NY):
        yy = lax.rem(y + d, NY)
        for h in range(NH):
            for pair in range(2):
                rhs[h, pair, yy] = rights[d][pair, h]
    for h in range(NH):
        total = None
        for pair in range(2):
            part = lax.dot_general(
                lhs[h, pair].reshape(NX * NC * ROWS, DEPTH),
                rhs[h, pair].reshape(NY * ROWS, DEPTH),
                (((1,), (1,)), ((), ())),
                preferred_element_type=jnp.float32,
            )
            total = part if total is None else total + part
        total = total.astype(BF16)
        for p in range(NZ):
            out[p, h] = total[p * ROWS : (p + 1) * ROWS]


def sum_kernel(place, pieces, out0, out1):
    x, y, c, z = (place[NH + i] for i in range(4))
    lane = lax.broadcasted_iota(jnp.int32, (1, DEPTH), 1)
    yy = lax.div(lane, ROWS)
    b = ((x * NY + yy) * NC + c) * ROWS + lax.rem(lane, ROWS)
    row = lax.broadcasted_iota(jnp.int32, (ROWS, 1), 0)
    a = ((lax.div(z, NC) * NY + y) * NC + lax.rem(z, NC)) * ROWS + row
    src = lax.broadcasted_iota(jnp.int32, (DEPTH, DEPTH), 0)
    dst = lax.broadcasted_iota(jnp.int32, (DEPTH, DEPTH), 1)
    want = lax.div(dst, NC * ROWS) * ROWS + lax.rem(dst, ROWS)
    mine = lax.rem(lax.div(dst, ROWS), NC) == c
    for k, out in enumerate((out0, out1)):
        half = lax.rem(c + k, 2)
        order = (mine & (src == want + half * HALF)).astype(BF16)
        for h in range(NH):
            total = pieces[0, h].astype(jnp.float32)
            for r in range(1, NZ):
                total = total + pieces[r, h].astype(jnp.float32)
            live = (a < place[h]) & (b < place[h])
            total = jnp.where(live, total, 0.0).astype(BF16)
            out[h] = jnp.dot(total, order, preferred_element_type=jnp.float32).astype(BF16)


def kernel(body, shapes, specs, scratch=(), flops=0):
    many = isinstance(shapes, list)
    make = lambda s: jax.ShapeDtypeStruct(s, BF16)
    return pl.pallas_call(
        body,
        out_shape=[make(s) for s in shapes] if many else make(shapes),
        in_specs=specs,
        out_specs=[VMEM] * len(shapes) if many else VMEM,
        scratch_shapes=[pltpu.VMEM(s, BF16) for s in scratch],
        compiler_params=PARAMS,
        cost_estimate=pl.CostEstimate(flops=flops, bytes_accessed=2**21, transcendentals=0),
    )


def shift(n, d):
    return [((i + d) % n, i) for i in range(n)]


def local(amplitudes, crossed, coulomb, exchange_int, block_order):
    place = [lax.axis_index(n) for n in ("x", "y", "c", "z")]
    place = jnp.concatenate([block_order, jnp.stack(place).astype(jnp.int32)])

    r = {0: jnp.stack([coulomb, exchange_int])}
    for d in (1, 2, 3):
        r[d] = lax.ppermute(r[d - 1], "y", shift(NY, 1))
        r[-d] = lax.ppermute(r[1 - d], "y", shift(NY, -1))
    r[4] = jnp.stack(
        [
            lax.ppermute(r[3][0], "y", shift(NY, 1)),
            lax.ppermute(r[-3][1], "y", shift(NY, -1)),
        ]
    )
    left = kernel(left_kernel, (NX,) + BLOCK, [SMEM, VMEM, VMEM, ANY])(
        place, amplitudes, crossed, r[0]
    )
    own = lax.all_to_all(left, "x", 0, 0, tiled=True)
    other = kernel(copy_kernel, (NX,) + BLOCK, [VMEM, ANY])(own, r[2])
    other = lax.ppermute(other, "c", shift(NC, 1))
    rights = [r[0], r[1], r[2], r[3], r[4], r[-3], r[-2], r[-1]]

    pieces = kernel(
        tile_kernel,
        (NZ,) + PIECE,
        [SMEM] + [VMEM] * (2 + NY),
        [(NH, 2, NX * NC, ROWS, DEPTH), (NH, 2, NY, ROWS, DEPTH)],
        flops=8 * NH * (NY * ROWS) ** 2 * DEPTH,
    )(place, own, other, *rights)
    pieces = lax.all_to_all(pieces, "z", 0, 0, tiled=True)
    halves = kernel(sum_kernel, [PIECE, PIECE], [SMEM, VMEM])(place, pieces)
    result = None
    for k, part in enumerate(halves):
        moves = []
        for x in range(NX):
            for c in range(NC):
                for z in range(NZ):
                    to = z * NZ + x * 2 + (c + k) % 2
                    moves.append(((x * NC + c) * NZ + z, to))
        part = lax.ppermute(part, ("x", "c", "z"), moves)
        result = part if result is None else result + part
    return result


def solution(mesh):
    grid = Mesh(mesh.devices.reshape(NX, NY, NC, NZ), ("x", "y", "c", "z"))
    spec = P(None, ("x", "y", "c"), "z")
    return jax.shard_map(
        local, mesh=grid, in_specs=(spec,) * 4 + (P(),), out_specs=spec, check_vma=False
    )
```

time: 124 us -> 111 us (0.90)
  the two profiles are of different devices: /device:TPU:6 before, /device:TPU:7 now
where the time goes in v2:
time: 111 us; the launch traced here: 110 us
  starting transfers between devices  46.8 us (42%)
  blocking collectives  31.7 us (29%)
  waiting for transfers between devices  24.3 us (22%)
  Pallas kernels  4.84 us (4%)
  other arithmetic  1.72 us (2%)
    all_to_all x1, blocking collectives, local(): pieces = lax.all_to_all(pieces, 'z', 0, 0, tiled=True)  31.7 us
    ppermute x3, starting transfers between devices, local(): r[d] = lax.ppermute(r[d - 1], 'y', shift(NY, 1))  15.1 us
    ppermute x2, waiting for transfers between devices, local(): part = lax.ppermute(part, ('x', 'c', 'z'), moves)  14.1 us
    ppermute x2, starting transfers between devices, local(): part = lax.ppermute(part, ('x', 'c', 'z'), moves)  8.44 us
    ppermute x3, starting transfers between devices, local(): r[-d] = lax.ppermute(r[1 - d], 'y', shift(NY, -1))  6.84 us
    ppermute x1, starting transfers between devices, local(): other = lax.ppermute(other, 'c', shift(NC, 1))  6.82 us
    ppermute x1, waiting for transfers between devices, local(): lax.ppermute(r[-3][1], 'y', shift(NY, -1))  4.76 us
    all_to_all x1, starting transfers between devices, local(): own = lax.all_to_all(left, 'x', 0, 0, tiled=True)  4.21 us
  transfers between devices with their start and end apart: 12, of which 7 were waited for; matrix products, arithmetic and copies ran while one was open for 0% of the time, Pallas kernels for 0%

profile of v2, /device:TPU:7, one launch (start us, length us, event | category | flops | bytes accessed | tf_op | source)
XLA Modules:
  0.0 110.3 jit_solution(10519964762941274674)
XLA Ops:
  0.0 0.0 copy-start
  0.0 0.0 copy-start.1
  0.0 1.0 pad_maximum_fusion._.refs_0_
  1.0 0.0 copy-start.2
  1.0 0.6 copy-done.2
  1.7 0.1 concatenate.3.place
  1.8 0.0 copy-done
  1.8 0.0 copy-done.1
  1.8 1.5 %shard_map.55 = bf16[4,2,3,48,384]{4,3,2,1,0:T(8,128)(2,1)} custom-call(s32[7]{0:T(128)S(1)} %concatenate.3.place, bf16[3,48,384]{2,1,0:T(8,128)(2,1)S(1)} %copy-done, bf16[3,48,384]{2,1,0:T(8,128)(2,1)S(1)} %copy-done.1, bf16[2,3,48,384]{3,2,1,0:T(8,128)(2,1)S(1)} %pad_maximum_fusion._.refs_0_), custom_call_target="tpu_custom_call" | custom-call | bytes 2097152 | tf_op jit(solution)/shard_map/pallas_call | solution.py:117
  3.3 4.2 %all-to-all-start = ((bf16[4,2,3,48,384]{4,3,2,1,0:T(8,128)(2,1)}), bf16[4,2,3,48,384]{4,3,2,1,0:T(8,128)(2,1)S(1)}, u32[]{:S(2)}, u32[]{:S(2)}) async-start(bf16[4,2,3,48,384]{4,3,2,1,0:T(8,128)(2,1)} %shard_map.55), calls=%async_computation | async-start | bytes 1769472 | tf_op jit(solution)/shard_map/all_to_all | solution.py:120
  7.5 5.1 %collective-permute-start = (bf16[2,3,48,384]{3,2,1,0:T(8,128)(2,1)S(1)}, bf16[2,3,48,384]{3,2,1,0:T(8,128)(2,1)S(1)}, u32[]{:S(2)}, u32[]{:S(2)}) collective-permute-start(bf16[2,3,48,384]{3,2,1,0:T(8,128)(2,1)S(1)} %pad_maximum_fusion._.refs_0_), channel_id=1, source_target_pairs={{16,0},{32,16},{48,32},{64,48},{80,64},{96,80},{112,96},{0,112},{1... | collective-permute-start | bytes 663560 | tf_op jit(solution)/shard_map/ppermute | solution.py:109
  12.6 1.9 %collective-permute-start.5 = (bf16[2,3,48,384]{3,2,1,0:T(8,128)(2,1)S(1)}, bf16[2,3,48,384]{3,2,1,0:T(8,128)(2,1)S(1)}, u32[]{:S(2)}, u32[]{:S(2)}) collective-permute-start(bf16[2,3,48,384]{3,2,1,0:T(8,128)(2,1)S(1)} %pad_maximum_fusion._.refs_0_), channel_id=1, source_target_pairs={{112,0},{0,16},{16,32},{32,48},{48,64},{64,80},{80,96},{96,112},{1... | collective-permute-start | bytes 663560 | tf_op jit(solution)/shard_map/ppermute | solution.py:110
  14.6 0.9 collective-permute-done.refs_1_
  15.5 5.0 %collective-permute-start.1 = (bf16[2,3,48,384]{3,2,1,0:T(8,128)(2,1)S(1)}, bf16[2,3,48,384]{3,2,1,0:T(8,128)(2,1)S(1)}, u32[]{:S(2)}, u32[]{:S(2)}) collective-permute-start(bf16[2,3,48,384]{3,2,1,0:T(8,128)(2,1)S(1)} %collective-permute-done.refs_1_), channel_id=1, source_target_pairs={{16,0},{32,16},{48,32},{64,48},{80,64},{96,80},{112,96},{0,112},{1... | collective-permute-start | bytes 663560 | tf_op jit(solution)/shard_map/ppermute | solution.py:109
  20.5 0.3 collective-permute-done.5.refs_7_
  20.8 1.9 %collective-permute-start.6 = (bf16[2,3,48,384]{3,2,1,0:T(8,128)(2,1)S(1)}, bf16[2,3,48,384]{3,2,1,0:T(8,128)(2,1)S(1)}, u32[]{:S(2)}, u32[]{:S(2)}) collective-permute-start(bf16[2,3,48,384]{3,2,1,0:T(8,128)(2,1)S(1)} %collective-permute-done.5.refs_7_), channel_id=1, source_target_pairs={{112,0},{0,16},{16,32},{32,48},{48,64},{64,80},{80,96},{96,112},{1... | collective-permute-start | bytes 663560 | tf_op jit(solution)/shard_map/ppermute | solution.py:110
  22.7 0.6 collective-permute-done.1._.refs_2_
  23.4 5.0 %collective-permute-start.3 = (bf16[2,3,48,384]{3,2,1,0:T(8,128)(2,1)S(1)}, bf16[2,3,48,384]{3,2,1,0:T(8,128)(2,1)S(1)}, u32[]{:S(2)}, u32[]{:S(2)}) collective-permute-start(bf16[2,3,48,384]{3,2,1,0:T(8,128)(2,1)S(1)} %collective-permute-done.1._.refs_2_), channel_id=1, source_target_pairs={{16,0},{32,16},{48,32},{64,48},{80,64},{96,80},{112,96},{0,112},{1... | collective-permute-start | bytes 663560 | tf_op jit(solution)/shard_map/ppermute | solution.py:109
  28.4 0.0 all-to-all-done.src.own
  28.4 0.1 shard_map.56
  28.5 6.8 %collective-permute-start.2 = (bf16[4,2,3,48,384]{4,3,2,1,0:T(8,128)(2,1)S(1)}, bf16[4,2,3,48,384]{4,3,2,1,0:T(8,128)(2,1)S(1)}, u32[]{:S(2)}, u32[]{:S(2)}) collective-permute-start(bf16[4,2,3,48,384]{4,3,2,1,0:T(8,128)(2,1)S(1)} %shard_map.56), channel_id=1, source_target_pairs={{8,0},{0,8},{9,1},{1,9},{10,2},{2,10},{11,3},{3,11},{12,4},{4,12},... | collective-permute-start | bytes 2654216 | tf_op jit(solution)/shard_map/ppermute | solution.py:122
  35.3 0.0 collective-permute-done.6.refs_6_
  35.3 3.0 %collective-permute-start.7 = (bf16[2,3,48,384]{3,2,1,0:T(8,128)(2,1)S(1)}, bf16[2,3,48,384]{3,2,1,0:T(8,128)(2,1)S(1)}, u32[]{:S(2)}, u32[]{:S(2)}) collective-permute-start(bf16[2,3,48,384]{3,2,1,0:T(8,128)(2,1)S(1)} %collective-permute-done.6.refs_6_), channel_id=1, source_target_pairs={{112,0},{0,16},{16,32},{32,48},{48,64},{64,80},{80,96},{96,112},{1... | collective-permute-start | bytes 663560 | tf_op jit(solution)/shard_map/ppermute | solution.py:110
  38.3 0.0 collective-permute-done.3.refs_3_
  38.4 3.5 %collective-permute-start.4 = (bf16[3,48,384]{2,1,0:T(8,128)(2,1)S(1)}, bf16[3,48,384]{2,1,0:T(8,128)(2,1)S(1)}, u32[]{:S(2)}, u32[]{:S(2)}) collective-permute-start(bf16[3,48,384]{2,1,0:T(8,128)(2,1)S(1)} %slice_bitcast_fusion.1), channel_id=1, source_target_pairs={{16,0},{32,16},{48,32},{64,48},{80,64},{96,80},{112,96},{0,112},{1... | collective-permute-start | bytes 331784 | tf_op jit(solution)/shard_map/ppermute | solution.py:113
  41.9 3.6 %collective-permute-done.7.refs_5_ = bf16[2,3,48,384]{3,2,1,0:T(8,128)(2,1)S(1)} collective-permute-done((bf16[2,3,48,384]{3,2,1,0:T(8,128)(2,1)S(1)}, bf16[2,3,48,384]{3,2,1,0:T(8,128)(2,1)S(1)}, u32[]{:S(2)}, u32[]{:S(2)}) %collective-permute-start.7) | collective-permute-done | bytes 221216 | tf_op jit(solution)/shard_map/ppermute | solution.py:110
  45.5 1.9 %collective-permute-start.8 = (bf16[3,48,384]{2,1,0:T(8,128)(2,1)S(1)}, bf16[3,48,384]{2,1,0:T(8,128)(2,1)S(1)}, u32[]{:S(2)}, u32[]{:S(2)}) collective-permute-start(bf16[3,48,384]{2,1,0:T(8,128)(2,1)S(1)} %slice_bitcast_fusion), channel_id=1, source_target_pairs={{112,0},{0,16},{16,32},{32,48},{48,64},{64,80},{80,96},{96,112},{1... | collective-permute-start | bytes 331784 | tf_op jit(solution)/shard_map/ppermute | solution.py:114
  47.4 0.0 collective-permute-done.4
  47.4 4.8 %collective-permute-done.8 = bf16[3,48,384]{2,1,0:T(8,128)(2,1)S(1)} collective-permute-done((bf16[3,48,384]{2,1,0:T(8,128)(2,1)S(1)}, bf16[3,48,384]{2,1,0:T(8,128)(2,1)S(1)}, u32[]{:S(2)}, u32[]{:S(2)}) %collective-permute-start.8) | collective-permute-done | bytes 110624 | tf_op jit(solution)/shard_map/ppermute | solution.py:114
  52.2 0.0 collective-permute-done.2.other
  52.2 2.1 %shard_map.57 = bf16[8,3,48,384]{3,2,1,0:T(8,128)(2,1)S(1)} custom-call(s32[7]{0:T(128)S(1)} %concatenate.3.place, bf16[4,2,3,48,384]{4,3,2,1,0:T(8,128)(2,1)S(1)} %all-to-all-done.src.own, bf16[4,2,3,48,384]{4,3,2,1,0:T(8,128)(2,1)S(1)} %collective-permute-done.2.other, bf16[2,3,48,384]{3,2,1,0:T(8,128)(2,1)S(1)} %pad_maximum_fusion._.refs_0_, ...), custom_call_target="tpu_custom_call" | custom-call | flops 1358954496 | bytes 2097152 | tf_op jit(solution)/shard_map/pallas_call | solution.py:125
  54.3 31.7 %all_to_all.10.pieces = bf16[8,3,48,384]{3,2,1,0:T(8,128)(2,1)S(1)} all-to-all(bf16[8,3,48,384]{3,2,1,0:T(8,128)(2,1)S(1)} %shard_map.57), channel_id=1, replica_groups=mesh['x'=4,'y'=8,'c'=2,'z'=8] {'z'}, dimensions={0} | all-to-all | bytes 1769472 | tf_op jit(solution)/shard_map/all_to_all | solution.py:132
  86.0 1.1 %shard_map.58 = (bf16[3,48,384]{2,1,0:T(8,128)(2,1)S(1)}, bf16[3,48,384]{2,1,0:T(8,128)(2,1)S(1)}) custom-call(s32[7]{0:T(128)S(1)} %concatenate.3.place, bf16[8,3,48,384]{3,2,1,0:T(8,128)(2,1)S(1)} %all_to_all.10.pieces), custom_call_target="tpu_custom_call" | custom-call | bytes 2097152 | tf_op jit(solution)/shard_map/pallas_call | solution.py:133
  87.2 5.5 %collective-permute-start.10 = (bf16[3,48,384]{2,1,0:T(8,128)(2,1)S(1)}, bf16[3,48,384]{2,1,0:T(8,128)(2,1)S(1)}, u32[]{:S(2)}, u32[]{:S(2)}) collective-permute-start(bf16[3,48,384]{2,1,0:T(8,128)(2,1)S(1)} %get-tuple-element.8), channel_id=1, source_target_pairs={{0,1},{1,9},{2,129},{3,137},{4,257},{5,265},{6,385},{7,393},{8,0},... | collective-permute-start | bytes 331784 | tf_op jit(solution)/shard_map/ppermute | solution.py:142
  92.6 3.0 %collective-permute-start.9 = (bf16[3,48,384]{2,1,0:T(8,128)(2,1)S(1)}, bf16[3,48,384]{2,1,0:T(8,128)(2,1)S(1)}, u32[]{:S(2)}, u32[]{:S(2)}) collective-permute-start(bf16[3,48,384]{2,1,0:T(8,128)(2,1)S(1)} %get-tuple-element.7), channel_id=1, source_target_pairs={{0,0},{1,8},{2,128},{3,136},{4,256},{5,264},{6,384},{7,392},{8,1},... | collective-permute-start | bytes 331784 | tf_op jit(solution)/shard_map/ppermute | solution.py:142
  95.6 4.2 %collective-permute-done.10 = bf16[3,48,384]{2,1,0:T(8,128)(2,1)S(1)} collective-permute-done((bf16[3,48,384]{2,1,0:T(8,128)(2,1)S(1)}, bf16[3,48,384]{2,1,0:T(8,128)(2,1)S(1)}, u32[]{:S(2)}, u32[]{:S(2)}) %collective-permute-start.10) | collective-permute-done | bytes 110624 | tf_op jit(solution)/shard_map/ppermute | solution.py:142
  99.8 9.9 %collective-permute-done.9 = bf16[3,48,384]{2,1,0:T(8,128)(2,1)S(1)} collective-permute-done((bf16[3,48,384]{2,1,0:T(8,128)(2,1)S(1)}, bf16[3,48,384]{2,1,0:T(8,128)(2,1)S(1)}, u32[]{:S(2)}, u32[]{:S(2)}) %collective-permute-start.9) | collective-permute-done | bytes 110624 | tf_op jit(solution)/shard_map/ppermute | solution.py:142
  109.7 0.7 add.3
  (3 shorter events, 0.1 us)
Async XLA Ops:
  0.0 1.8 %copy-start = (bf16[3,48,384]{2,1,0:T(8,128)(2,1)S(1)}, bf16[3,48,384]{2,1,0:T(8,128)(2,1)}, u32[]{:S(2)}) copy-start(bf16[3,48,384]{2,1,0:T(8,128)(2,1)} %amp.1) | copy-start | bytes 331780
  0.0 1.8 %copy-start.1 = (bf16[3,48,384]{2,1,0:T(8,128)(2,1)S(1)}, bf16[3,48,384]{2,1,0:T(8,128)(2,1)}, u32[]{:S(2)}) copy-start(bf16[3,48,384]{2,1,0:T(8,128)(2,1)} %cross.1) | copy-start | bytes 331780
  1.0 0.7 copy-start.2
  3.3 25.1 %all-to-all-start = ((bf16[4,2,3,48,384]{4,3,2,1,0:T(8,128)(2,1)}), bf16[4,2,3,48,384]{4,3,2,1,0:T(8,128)(2,1)S(1)}, u32[]{:S(2)}, u32[]{:S(2)}) async-start(bf16[4,2,3,48,384]{4,3,2,1,0:T(8,128)(2,1)} %shard_map.55), calls=%async_computation | async-start | bytes 1769472 | tf_op jit(solution)/shard_map/all_to_all | solution.py:120
  7.5 7.9 %collective-permute-start = (bf16[2,3,48,384]{3,2,1,0:T(8,128)(2,1)S(1)}, bf16[2,3,48,384]{3,2,1,0:T(8,128)(2,1)S(1)}, u32[]{:S(2)}, u32[]{:S(2)}) collective-permute-start(bf16[2,3,48,384]{3,2,1,0:T(8,128)(2,1)S(1)} %pad_maximum_fusion._.refs_0_), channel_id=1, source_target_pairs={{16,0},{32,16},{48,32},{64,48},{80,64},{96,80},{112,96},{0,112},{1... | collective-permute-start | bytes 663560 | tf_op jit(solution)/shard_map/ppermute | solution.py:109
  12.6 8.2 %collective-permute-start.5 = (bf16[2,3,48,384]{3,2,1,0:T(8,128)(2,1)S(1)}, bf16[2,3,48,384]{3,2,1,0:T(8,128)(2,1)S(1)}, u32[]{:S(2)}, u32[]{:S(2)}) collective-permute-start(bf16[2,3,48,384]{3,2,1,0:T(8,128)(2,1)S(1)} %pad_maximum_fusion._.refs_0_), channel_id=1, source_target_pairs={{112,0},{0,16},{16,32},{32,48},{48,64},{64,80},{80,96},{96,112},{1... | collective-permute-start | bytes 663560 | tf_op jit(solution)/shard_map/ppermute | solution.py:110
  15.5 7.9 %collective-permute-start.1 = (bf16[2,3,48,384]{3,2,1,0:T(8,128)(2,1)S(1)}, bf16[2,3,48,384]{3,2,1,0:T(8,128)(2,1)S(1)}, u32[]{:S(2)}, u32[]{:S(2)}) collective-permute-start(bf16[2,3,48,384]{3,2,1,0:T(8,128)(2,1)S(1)} %collective-permute-done.refs_1_), channel_id=1, source_target_pairs={{16,0},{32,16},{48,32},{64,48},{80,64},{96,80},{112,96},{0,112},{1... | collective-permute-start | bytes 663560 | tf_op jit(solution)/shard_map/ppermute | solution.py:109
  20.8 14.5 %collective-permute-start.6 = (bf16[2,3,48,384]{3,2,1,0:T(8,128)(2,1)S(1)}, bf16[2,3,48,384]{3,2,1,0:T(8,128)(2,1)S(1)}, u32[]{:S(2)}, u32[]{:S(2)}) collective-permute-start(bf16[2,3,48,384]{3,2,1,0:T(8,128)(2,1)S(1)} %collective-permute-done.5.refs_7_), channel_id=1, source_target_pairs={{112,0},{0,16},{16,32},{32,48},{48,64},{64,80},{80,96},{96,112},{1... | collective-permute-start | bytes 663560 | tf_op jit(solution)/shard_map/ppermute | solution.py:110
  23.4 15.0 %collective-permute-start.3 = (bf16[2,3,48,384]{3,2,1,0:T(8,128)(2,1)S(1)}, bf16[2,3,48,384]{3,2,1,0:T(8,128)(2,1)S(1)}, u32[]{:S(2)}, u32[]{:S(2)}) collective-permute-start(bf16[2,3,48,384]{3,2,1,0:T(8,128)(2,1)S(1)} %collective-permute-done.1._.refs_2_), channel_id=1, source_target_pairs={{16,0},{32,16},{48,32},{64,48},{80,64},{96,80},{112,96},{0,112},{1... | collective-permute-start | bytes 663560 | tf_op jit(solution)/shard_map/ppermute | solution.py:109
  28.5 23.7 %collective-permute-start.2 = (bf16[4,2,3,48,384]{4,3,2,1,0:T(8,128)(2,1)S(1)}, bf16[4,2,3,48,384]{4,3,2,1,0:T(8,128)(2,1)S(1)}, u32[]{:S(2)}, u32[]{:S(2)}) collective-permute-start(bf16[4,2,3,48,384]{4,3,2,1,0:T(8,128)(2,1)S(1)} %shard_map.56), channel_id=1, source_target_pairs={{8,0},{0,8},{9,1},{1,9},{10,2},{2,10},{11,3},{3,11},{12,4},{4,12},... | collective-permute-start | bytes 2654216 | tf_op jit(solution)/shard_map/ppermute | solution.py:122
  35.3 10.2 %collective-permute-start.7 = (bf16[2,3,48,384]{3,2,1,0:T(8,128)(2,1)S(1)}, bf16[2,3,48,384]{3,2,1,0:T(8,128)(2,1)S(1)}, u32[]{:S(2)}, u32[]{:S(2)}) collective-permute-start(bf16[2,3,48,384]{3,2,1,0:T(8,128)(2,1)S(1)} %collective-permute-done.6.refs_6_), channel_id=1, source_target_pairs={{112,0},{0,16},{16,32},{32,48},{48,64},{64,80},{80,96},{96,112},{1... | collective-permute-start | bytes 663560 | tf_op jit(solution)/shard_map/ppermute | solution.py:110
  38.4 9.0 %collective-permute-start.4 = (bf16[3,48,384]{2,1,0:T(8,128)(2,1)S(1)}, bf16[3,48,384]{2,1,0:T(8,128)(2,1)S(1)}, u32[]{:S(2)}, u32[]{:S(2)}) collective-permute-start(bf16[3,48,384]{2,1,0:T(8,128)(2,1)S(1)} %slice_bitcast_fusion.1), channel_id=1, source_target_pairs={{16,0},{32,16},{48,32},{64,48},{80,64},{96,80},{112,96},{0,112},{1... | collective-permute-start | bytes 331784 | tf_op jit(solution)/shard_map/ppermute | solution.py:113
  45.5 6.7 %collective-permute-start.8 = (bf16[3,48,384]{2,1,0:T(8,128)(2,1)S(1)}, bf16[3,48,384]{2,1,0:T(8,128)(2,1)S(1)}, u32[]{:S(2)}, u32[]{:S(2)}) collective-permute-start(bf16[3,48,384]{2,1,0:T(8,128)(2,1)S(1)} %slice_bitcast_fusion), channel_id=1, source_target_pairs={{112,0},{0,16},{16,32},{32,48},{48,64},{64,80},{80,96},{96,112},{1... | collective-permute-start | bytes 331784 | tf_op jit(solution)/shard_map/ppermute | solution.py:114
  87.2 12.7 %collective-permute-start.10 = (bf16[3,48,384]{2,1,0:T(8,128)(2,1)S(1)}, bf16[3,48,384]{2,1,0:T(8,128)(2,1)S(1)}, u32[]{:S(2)}, u32[]{:S(2)}) collective-permute-start(bf16[3,48,384]{2,1,0:T(8,128)(2,1)S(1)} %get-tuple-element.8), channel_id=1, source_target_pairs={{0,1},{1,9},{2,129},{3,137},{4,257},{5,265},{6,385},{7,393},{8,0},... | collective-permute-start | bytes 331784 | tf_op jit(solution)/shard_map/ppermute | solution.py:142
  92.6 17.0 %collective-permute-start.9 = (bf16[3,48,384]{2,1,0:T(8,128)(2,1)S(1)}, bf16[3,48,384]{2,1,0:T(8,128)(2,1)S(1)}, u32[]{:S(2)}, u32[]{:S(2)}) collective-permute-start(bf16[3,48,384]{2,1,0:T(8,128)(2,1)S(1)} %get-tuple-element.7), channel_id=1, source_target_pairs={{0,0},{1,8},{2,128},{3,136},{4,256},{5,264},{6,384},{7,392},{8,1},... | collective-permute-start | bytes 331784 | tf_op jit(solution)/shard_map/ppermute | solution.py:142

commit v3 on v1

v3 whole, which is shorter than its diff:
```python
import jax
import jax.numpy as jnp
from jax import lax
from jax.experimental import pallas as pl
from jax.experimental.pallas import tpu as pltpu
from jax.sharding import Mesh, PartitionSpec as P

NX, NF, NQ, NC, NZ = 4, 2, 4, 2, 8
AXES = ("x", "f", "q", "c", "z")
NH, ROWS, DEPTH = 3, 48, 384
BLOCK = (2, NH, ROWS, DEPTH)
PIECE = (NH, ROWS, DEPTH)
NP = NQ * NC
LANES = 128
LAST = 2 * ROWS
KEPT = LANES - LAST
LEFT = ROWS - KEPT
GROUP = 8
PACKED = (ROWS + GROUP, LANES)
VMEM = pl.BlockSpec(memory_space=pltpu.VMEM)
SMEM = pl.BlockSpec(memory_space=pltpu.SMEM)
PARAMS = pltpu.CompilerParams(vmem_limit_bytes=32 * 2**20)
BF16 = jnp.bfloat16


def left_kernel(place, amp, cross, out):
    k = place[NH + 4] * DEPTH + lax.broadcasted_iota(jnp.int32, (1, DEPTH), 1)
    for h in range(NH):
        live = k < place[h]
        for pair, ref in enumerate((amp, cross)):
            block = jnp.where(live, ref[h], jnp.zeros_like(ref[h]))
            out[pair, h] = block


def tile_kernel(place, own, other, near, far, out, lhs, rhs):
    f, c = place[NH + 1], place[NH + 3]
    for q in range(NQ):
        for h in range(NH):
            for pair in range(2):
                lhs[h, pair, 2 * q + c] = own[q, pair, h]
                lhs[h, pair, 2 * q + 1 - c] = other[q, pair, h]
    for x in range(NX):
        for h in range(NH):
            for pair in range(2):
                rhs[h, pair, 2 * x + f] = near[x, pair, h]
                rhs[h, pair, 2 * x + 1 - f] = far[x, pair, h]
    totals = []
    for h in range(NH):
        total = None
        for pair in range(2):
            part = lax.dot_general(
                lhs[h, pair].reshape(NP * ROWS, DEPTH),
                rhs[h, pair].reshape(NZ * ROWS, DEPTH),
                (((1,), (1,)), ((), ())),
                preferred_element_type=jnp.float32,
            )
            total = part if total is None else total + part
        totals.append(total)
    fill = jnp.zeros((GROUP, LANES - ROWS // GROUP * LEFT), jnp.float32)
    for p in range(NP):
        rows = [t[p * ROWS : (p + 1) * ROWS] for t in totals]
        for z in range(NZ):
            at = z * ROWS
            main = jnp.concatenate(
                [rows[0][:, at : at + ROWS], rows[1][:, at : at + ROWS], rows[2][:, at : at + KEPT]], axis=1
            )
            rest = rows[2][:, at + KEPT : at + ROWS]
            rest = [rest[g : g + GROUP] for g in range(0, ROWS, GROUP)]
            rest = jnp.concatenate(rest + [fill], axis=1)
            out[p * NZ + z] = jnp.concatenate([main, rest], axis=0).astype(BF16)


def sum_kernel(place, pieces, out):
    x, f, q, c, z = (place[NH + i] for i in range(5))
    straight = lax.rem(z, 2) == f
    sums = []
    for s in range(NP):
        total = pieces[s * NZ].astype(jnp.float32)
        for r in range(1, NZ):
            total = total + pieces[s * NZ + r].astype(jnp.float32)
        sums.append(total)
    b = z * DEPTH + lax.broadcasted_iota(jnp.int32, (1, DEPTH), 1)
    a = (((x * NF + f) * NQ + q) * NC + c) * ROWS + lax.broadcasted_iota(jnp.int32, (ROWS, 1), 0)
    blocks = [[] for _ in range(NH)]
    for s in range(NP):
        mirrored = (NQ - 1 - s // NC) * NC + s % NC
        total = jnp.where(straight, sums[s], sums[mirrored])
        rest = [total[ROWS:, g * LEFT : (g + 1) * LEFT] for g in range(ROWS // GROUP)]
        rest = jnp.concatenate(rest, axis=0)
        blocks[0].append(total[:ROWS, :ROWS])
        blocks[1].append(total[:ROWS, ROWS:LAST])
        blocks[2].append(jnp.concatenate([total[:ROWS, LAST:], rest], axis=1))
    for h in range(NH):
        live = (a < place[h]) & (b < place[h])
        whole = jnp.concatenate(blocks[h], axis=1)
        out[h] = jnp.where(live, whole, 0.0).astype(BF16)


def kernel(body, shape, specs, scratch=(), flops=0):
    return pl.pallas_call(
        body,
        out_shape=jax.ShapeDtypeStruct(shape, BF16),
        in_specs=specs,
        out_specs=VMEM,
        scratch_shapes=[pltpu.VMEM(s, BF16) for s in scratch],
        compiler_params=PARAMS,
        cost_estimate=pl.CostEstimate(flops=flops, bytes_accessed=2**21, transcendentals=0),
    )


def local(amplitudes, crossed, coulomb, exchange_int, block_order):
    place = [lax.axis_index(n) for n in AXES]
    place = jnp.concatenate([block_order, jnp.stack(place).astype(jnp.int32)])

    def along_x(block):
        return lax.all_to_all(jnp.broadcast_to(block, (NX,) + BLOCK), "x", 0, 0, tiled=True)

    right = jnp.stack([coulomb, exchange_int])
    n = NF * NQ
    mirror = lax.ppermute(right, ("f", "q"), [(i, n - 1 - i) for i in range(n)])
    near = along_x(right)
    left = kernel(left_kernel, BLOCK, [SMEM, VMEM, VMEM])(place, amplitudes, crossed)
    own = lax.all_gather(left, "q")
    far = along_x(mirror)
    other = lax.ppermute(own, "c", [(0, 1), (1, 0)])
    pieces = kernel(
        tile_kernel,
        (NP * NZ,) + PACKED,
        [SMEM] + [VMEM] * 4,
        [(NH, 2, NP, ROWS, DEPTH), (NH, 2, NZ, ROWS, DEPTH)],
        flops=8 * NH * (NP * ROWS) ** 2 * DEPTH,
    )(place, own, other, near, far)
    pieces = lax.all_to_all(pieces, ("q", "c", "z"), 0, 0, tiled=True)
    return kernel(sum_kernel, PIECE, [SMEM, VMEM])(place, pieces)


def solution(mesh):
    grid = Mesh(mesh.devices.reshape(NX, NF, NQ, NC, NZ), AXES)
    spec = P(None, AXES[:4], "z")
    return jax.shard_map(
        local, mesh=grid, in_specs=(spec,) * 4 + (P(),), out_specs=spec, check_vma=False
    )
```

time: 124 us -> 98.4 us (0.79)
  the two profiles are of different devices: /device:TPU:6 before, /device:TPU:57 now
where the time goes in v3:
time: 98.4 us; the launch traced here: 98.1 us
  blocking collectives  81 us (82%)
  starting transfers between devices  9.56 us (10%)
  Pallas kernels  4.61 us (5%)
  local copies, waits for them, and re-layouts  1.81 us (2%)
    all_to_all x1, blocking collectives, local(): pieces = lax.all_to_all(pieces, ('q', 'c', 'z'), 0, 0, tiled=True)  40 us
    all_gather x1, blocking collectives, local(): own = lax.all_gather(left, 'q')  23.5 us
    all_to_all x1, blocking collectives, along_x(): lax.all_to_all(jnp.broadcast_to(block, (NX,) + BLOCK), 'x', 0, 0, tiled=T...  17.5 us
    all_to_all x1, starting transfers between devices, along_x(): lax.all_to_all(jnp.broadcast_to(block, (NX,) + BLOCK), 'x', 0, 0, tiled=T...  4.14 us
    ppermute x1, starting transfers between devices, local(): other = lax.ppermute(own, 'c', [(0, 1), (1, 0)])  3.5 us
    pallas_call x1, Pallas kernels, local(): kernel(tile_kernel, (NP * NZ,) + PACKED, [SMEM] + [VMEM] * 4, [(NH, 2, NP...  2.5 us
  transfers between devices with their start and end apart: 3, of which 0 were waited for; matrix products, arithmetic and copies ran while one was open for 0% of the time, Pallas kernels for 1%

profile of v3, /device:TPU:57, one launch (start us, length us, event | category | flops | bytes accessed | tf_op | source)
XLA Modules:
  0.0 98.1 jit_solution(6306889373534332209)
XLA Ops:
  0.0 1.0 pad_maximum_fusion
  1.0 1.0 %broadcast_in_dim.6 = bf16[4,2,3,48,384]{4,3,2,1,0:T(8,128)(2,1)} broadcast(bf16[2,3,48,384]{3,2,1,0:T(8,128)(2,1)S(1)} %pad_maximum_fusion), dimensions={1,2,3,4} | broadcast | bytes 1105920 | tf_op jit(solution)/shard_map/broadcast_in_dim | solution.py:116
  2.0 0.0 copy-start
  2.0 0.0 copy-start.1
  2.0 4.1 %all-to-all-start = ((bf16[4,2,3,48,384]{4,3,2,1,0:T(8,128)(2,1)}), bf16[4,2,3,48,384]{4,3,2,1,0:T(8,128)(2,1)S(1)}, u32[]{:S(2)}, u32[]{:S(2)}) async-start(bf16[4,2,3,48,384]{4,3,2,1,0:T(8,128)(2,1)} %broadcast_in_dim.6), calls=%async_computation | async-start | bytes 1769472 | tf_op jit(solution)/shard_map/all_to_all | solution.py:116
  6.1 1.9 %collective-permute-start.1 = (bf16[2,3,48,384]{3,2,1,0:T(8,128)(2,1)S(1)}, bf16[2,3,48,384]{3,2,1,0:T(8,128)(2,1)S(1)}, u32[]{:S(2)}, u32[]{:S(2)}) collective-permute-start(bf16[2,3,48,384]{3,2,1,0:T(8,128)(2,1)S(1)} %pad_maximum_fusion), channel_id=1, source_target_pairs={{0,112},{16,96},{32,80},{48,64},{64,48},{80,32},{96,16},{112,0},{1... | collective-permute-start | bytes 663560 | tf_op jit(solution)/shard_map/ppermute | solution.py:120
  8.0 0.0 copy-start.2
  8.1 0.6 copy-done.2
  8.7 0.1 concatenate.3.place
  8.8 0.0 copy-done
  8.8 0.0 copy-done.1
  8.8 0.6 shard_map.55
  9.4 23.5 %all-gather = bf16[8,3,48,384]{3,2,1,0:T(8,128)(2,1)S(1)} all-gather(bf16[2,3,48,384]{3,2,1,0:T(8,128)(2,1)S(1)} %shard_map.55), channel_id=2, replica_groups=mesh['x'=4,'f'=2,'q'=4,'c'=2,'z'=8] {'q'}, dimensions={0}, use_global_device_ids=true | all-gather | bytes 1105920 | tf_op jit(solution)/shard_map/all_gather | solution.py:123
  32.9 3.5 %collective-permute-start = (bf16[4,2,3,48,384]{4,3,2,1,0:T(8,128)(2,1)S(1)}, bf16[4,2,3,48,384]{4,3,2,1,0:T(8,128)(2,1)S(1)}, u32[]{:S(2)}, u32[]{:S(2)}) collective-permute-start(bf16[4,2,3,48,384]{4,3,2,1,0:T(8,128)(2,1)S(1)} %bitcast.8), channel_id=1, source_target_pairs={{0,8},{8,0},{1,9},{9,1},{2,10},{10,2},{3,11},{11,3},{4,12},{12,4},... | collective-permute-start | bytes 2654216 | tf_op jit(solution)/shard_map/ppermute | solution.py:125
  36.4 0.0 collective-permute-done.1
  36.4 0.0 all-to-all-done.near
  36.4 0.1 broadcast_in_dim.7
  36.5 17.5 %all_to_all.15.far = bf16[4,2,3,48,384]{4,3,2,1,0:T(8,128)(2,1)S(1)} all-to-all(bf16[4,2,3,48,384]{4,3,2,1,0:T(8,128)(2,1)S(1)} %broadcast_in_dim.7), channel_id=1, replica_groups=mesh['x'=4,'f'=2,'q'=4,'c'=2,'z'=8] {'x'}, dimensions={0} | all-to-all | bytes 1769472 | tf_op jit(solution)/shard_map/all_to_all | solution.py:116
  54.0 0.0 collective-permute-done.other
  54.0 2.5 %shard_map.56 = bf16[64,56,128]{2,1,0:T(8,128)(2,1)S(1)} custom-call(s32[8]{0:T(128)S(1)} %concatenate.3.place, bf16[4,2,3,48,384]{4,3,2,1,0:T(8,128)(2,1)S(1)} %bitcast.9, bf16[4,2,3,48,384]{4,3,2,1,0:T(8,128)(2,1)S(1)} %collective-permute-done.other, bf16[4,2,3,48,384]{4,3,2,1,0:T(8,128)(2,1)S(1)} %all-to-all-done.near, ...), custom_call_target="tpu_custom_call" | custom-call | flops 1358954496 | bytes 2097152 | tf_op jit(solution)/shard_map/pallas_call | solution.py:126
  56.5 40.0 %all_to_all.16.pieces = bf16[64,56,128]{2,1,0:T(8,128)(2,1)S(1)} all-to-all(bf16[64,56,128]{2,1,0:T(8,128)(2,1)S(1)} %shard_map.56), channel_id=1, replica_groups=mesh['x'=4,'f'=2,'q'=4,'c'=2,'z'=8] {'q','c','z'}, dimensions={0} | all-to-all | bytes 1835008 | tf_op jit(solution)/shard_map/all_to_all | solution.py:133
  96.6 1.5 %shard_map.57 = bf16[3,48,384]{2,1,0:T(8,128)(2,1)} custom-call(s32[8]{0:T(128)S(1)} %concatenate.3.place, bf16[64,56,128]{2,1,0:T(8,128)(2,1)S(1)} %all_to_all.16.pieces), custom_call_target="tpu_custom_call" | custom-call | bytes 2097152 | tf_op jit(solution)/shard_map/pallas_call | solution.py:134
Async XLA Ops:
  2.0 6.8 %copy-start = (bf16[3,48,384]{2,1,0:T(8,128)(2,1)S(1)}, bf16[3,48,384]{2,1,0:T(8,128)(2,1)}, u32[]{:S(2)}) copy-start(bf16[3,48,384]{2,1,0:T(8,128)(2,1)} %amp.1) | copy-start | bytes 331780
  2.0 6.8 %copy-start.1 = (bf16[3,48,384]{2,1,0:T(8,128)(2,1)S(1)}, bf16[3,48,384]{2,1,0:T(8,128)(2,1)}, u32[]{:S(2)}) copy-start(bf16[3,48,384]{2,1,0:T(8,128)(2,1)} %cross.1) | copy-start | bytes 331780
  2.0 34.4 %all-to-all-start = ((bf16[4,2,3,48,384]{4,3,2,1,0:T(8,128)(2,1)}), bf16[4,2,3,48,384]{4,3,2,1,0:T(8,128)(2,1)S(1)}, u32[]{:S(2)}, u32[]{:S(2)}) async-start(bf16[4,2,3,48,384]{4,3,2,1,0:T(8,128)(2,1)} %broadcast_in_dim.6), calls=%async_computation | async-start | bytes 1769472 | tf_op jit(solution)/shard_map/all_to_all | solution.py:116
  6.1 30.3 %collective-permute-start.1 = (bf16[2,3,48,384]{3,2,1,0:T(8,128)(2,1)S(1)}, bf16[2,3,48,384]{3,2,1,0:T(8,128)(2,1)S(1)}, u32[]{:S(2)}, u32[]{:S(2)}) collective-permute-start(bf16[2,3,48,384]{3,2,1,0:T(8,128)(2,1)S(1)} %pad_maximum_fusion), channel_id=1, source_target_pairs={{0,112},{16,96},{32,80},{48,64},{64,48},{80,32},{96,16},{112,0},{1... | collective-permute-start | bytes 663560 | tf_op jit(solution)/shard_map/ppermute | solution.py:120
  8.0 0.7 copy-start.2
  32.9 21.2 %collective-permute-start = (bf16[4,2,3,48,384]{4,3,2,1,0:T(8,128)(2,1)S(1)}, bf16[4,2,3,48,384]{4,3,2,1,0:T(8,128)(2,1)S(1)}, u32[]{:S(2)}, u32[]{:S(2)}) collective-permute-start(bf16[4,2,3,48,384]{4,3,2,1,0:T(8,128)(2,1)S(1)} %bitcast.8), channel_id=1, source_target_pairs={{0,8},{8,0},{1,9},{9,1},{2,10},{10,2},{3,11},{11,3},{4,12},{12,4},... | collective-permute-start | bytes 2654216 | tf_op jit(solution)/shard_map/ppermute | solution.py:125

commit v4 on v3

--- a/solution.py
+++ b/solution.py
@@ -18,27 +18,40 @@
 GROUP = 8
 PACKED = (ROWS + GROUP, LANES)
 VMEM = pl.BlockSpec(memory_space=pltpu.VMEM)
+ANY = pl.BlockSpec(memory_space=pl.ANY)
 SMEM = pl.BlockSpec(memory_space=pltpu.SMEM)
 PARAMS = pltpu.CompilerParams(vmem_limit_bytes=32 * 2**20)
 BF16 = jnp.bfloat16
 
 
-def left_kernel(place, amp, cross, out):
+def spread_kernel(mirror, amp, cross, _, spread, left):
+    for e in range(NX):
+        spread[e] = mirror[...]
+    left[0] = amp[...]
+    left[1] = cross[...]
+
+
+def mask_kernel(place, rows, _, out):
     k = place[NH + 4] * DEPTH + lax.broadcasted_iota(jnp.int32, (1, DEPTH), 1)
     for h in range(NH):
         live = k < place[h]
-        for pair, ref in enumerate((amp, cross)):
-            block = jnp.where(live, ref[h], jnp.zeros_like(ref[h]))
-            out[pair, h] = block
+        for q in range(NQ):
+            for pair in range(2):
+                block = rows[q, pair, h]
+                out[q, pair, h] = jnp.where(live, block, jnp.zeros_like(block))
 
 
-def tile_kernel(place, own, other, near, far, out, lhs, rhs):
+def tile_kernel(place, rows, near, far, *rest):
+    before, (out, lhs, rhs) = rest[:-3], rest[-3:]
     f, c = place[NH + 1], place[NH + 3]
+    if before:
+        for q in range(NQ):
+            for z in range(NZ):
+                out[(q * NC + c) * NZ + z] = before[0][q * NZ + z]
     for q in range(NQ):
         for h in range(NH):
             for pair in range(2):
-                lhs[h, pair, 2 * q + c] = own[q, pair, h]
-                lhs[h, pair, 2 * q + 1 - c] = other[q, pair, h]
+                lhs[h, pair, q] = rows[q, pair, h]
     for x in range(NX):
         for h in range(NH):
             for pair in range(2):
@@ -49,7 +62,7 @@
         total = None
         for pair in range(2):
             part = lax.dot_general(
-                lhs[h, pair].reshape(NP * ROWS, DEPTH),
+                lhs[h, pair].reshape(NQ * ROWS, DEPTH),
                 rhs[h, pair].reshape(NZ * ROWS, DEPTH),
                 (((1,), (1,)), ((), ())),
                 preferred_element_type=jnp.float32,
@@ -57,7 +70,7 @@
             total = part if total is None else total + part
         totals.append(total)
     fill = jnp.zeros((GROUP, LANES - ROWS // GROUP * LEFT), jnp.float32)
-    for p in range(NP):
+    for p in range(NQ):
         rows = [t[p * ROWS : (p + 1) * ROWS] for t in totals]
         for z in range(NZ):
             at = z * ROWS
@@ -67,7 +80,7 @@
             rest = rows[2][:, at + KEPT : at + ROWS]
             rest = [rest[g : g + GROUP] for g in range(0, ROWS, GROUP)]
             rest = jnp.concatenate(rest + [fill], axis=1)
-            out[p * NZ + z] = jnp.concatenate([main, rest], axis=0).astype(BF16)
+            out[((p * NC + 1 - c) if before else p) * NZ + z] = jnp.concatenate([main, rest], axis=0).astype(BF16)
 
 
 def sum_kernel(place, pieces, out):
@@ -96,13 +109,15 @@
         out[h] = jnp.where(live, whole, 0.0).astype(BF16)
 
 
-def kernel(body, shape, specs, scratch=(), flops=0):
+def kernel(body, shapes, specs, scratch=(), flops=0):
+    make = lambda shape: jax.ShapeDtypeStruct(shape, BF16)
+    many = isinstance(shapes, list)
     return pl.pallas_call(
         body,
-        out_shape=jax.ShapeDtypeStruct(shape, BF16),
+        out_shape=[make(shape) for shape in shapes] if many else make(shapes),
         in_specs=specs,
-        out_specs=VMEM,
-        scratch_shapes=[pltpu.VMEM(s, BF16) for s in scratch],
+        out_specs=[VMEM] * len(shapes) if many else VMEM,
+        scratch_shapes=[pltpu.VMEM(shape, BF16) for shape in scratch],
         compiler_params=PARAMS,
         cost_estimate=pl.CostEstimate(flops=flops, bytes_accessed=2**21, transcendentals=0),
     )
@@ -112,24 +127,28 @@
     place = [lax.axis_index(n) for n in AXES]
     place = jnp.concatenate([block_order, jnp.stack(place).astype(jnp.int32)])
 
-    def along_x(block):
-        return lax.all_to_all(jnp.broadcast_to(block, (NX,) + BLOCK), "x", 0, 0, tiled=True)
-
     right = jnp.stack([coulomb, exchange_int])
     n = NF * NQ
     mirror = lax.ppermute(right, ("f", "q"), [(i, n - 1 - i) for i in range(n)])
-    near = along_x(right)
-    left = kernel(left_kernel, BLOCK, [SMEM, VMEM, VMEM])(place, amplitudes, crossed)
+    near = lax.all_gather(right, "x")
+    spread, left = kernel(spread_kernel, [(NX,) + BLOCK, BLOCK], [VMEM] * 3 + [ANY])(
+        mirror, amplitudes, crossed, near
+    )
+    far = lax.all_to_all(spread, "x", 0, 0, tiled=True)
     own = lax.all_gather(left, "q")
-    far = along_x(mirror)
+    own = kernel(mask_kernel, (NQ,) + BLOCK, [SMEM, VMEM, ANY])(place, own, far)
     other = lax.ppermute(own, "c", [(0, 1), (1, 0)])
-    pieces = kernel(
-        tile_kernel,
-        (NP * NZ,) + PACKED,
-        [SMEM] + [VMEM] * 4,
-        [(NH, 2, NP, ROWS, DEPTH), (NH, 2, NZ, ROWS, DEPTH)],
-        flops=8 * NH * (NP * ROWS) ** 2 * DEPTH,
-    )(place, own, other, near, far)
+    pieces = []
+    for rows, count in ((own, NQ * NZ), (other, NP * NZ)):
+        pieces = kernel(
+            tile_kernel,
+            (count,) + PACKED,
+            [SMEM] + [VMEM] * (3 + len(pieces)),
+            [(NH, 2, NQ, ROWS, DEPTH), (NH, 2, NZ, ROWS, DEPTH)],
+            flops=4 * NH * (NP * ROWS) ** 2 * DEPTH,
+        )(place, rows, near, far, *pieces)
+        pieces = [pieces]
+    pieces = pieces[0]
     pieces = lax.all_to_all(pieces, ("q", "c", "z"), 0, 0, tiled=True)
     return kernel(sum_kernel, PIECE, [SMEM, VMEM])(place, pieces)
 

time: 98.4 us -> 94.6 us (0.961)
  the two profiles are of different devices: /device:TPU:57 before, /device:TPU:6 now
where the time goes in v4:
time: 94.6 us; the launch traced here: 93.9 us
  blocking collectives  71.8 us (76%)
  starting transfers between devices  13 us (14%)
  Pallas kernels  6.65 us (7%)
  other arithmetic  0.98 us (1%)
    all_to_all x1, blocking collectives, local(): pieces = lax.all_to_all(pieces, ('q', 'c', 'z'), 0, 0, tiled=True)  39.2 us
    all_gather x1, blocking collectives, local(): own = lax.all_gather(left, 'q')  17.9 us
    all_gather x1, blocking collectives, local(): near = lax.all_gather(right, 'x')  14.7 us
    all_to_all x1, starting transfers between devices, local(): far = lax.all_to_all(spread, 'x', 0, 0, tiled=True)  5.53 us
    ppermute x1, starting transfers between devices, local(): mirror = lax.ppermute(right, ('f', 'q'), [(i, n - 1 - i) for i in range(n)])  5.51 us
    pallas_call x2, Pallas kernels, local(): kernel(tile_kernel, (count,) + PACKED, [SMEM] + [VMEM] * (3 + len(pieces)...  3.44 us
    ppermute x1, starting transfers between devices, local(): other = lax.ppermute(own, 'c', [(0, 1), (1, 0)])  1.92 us
  transfers between devices with their start and end apart: 3, of which 1 were waited for; matrix products, arithmetic and copies ran while one was open for 0% of the time, Pallas kernels for 2%

profile of v4, /device:TPU:6, one launch (start us, length us, event | category | flops | bytes accessed | tf_op | source)
XLA Modules:
  0.0 93.9 jit_solution(2076275900145842657)
XLA Ops:
  0.0 1.0 %pad_maximum_fusion = bf16[2,3,48,384]{3,2,1,0:T(8,128)(2,1)S(1)} fusion(bf16[1,3,48,384]{3,2,1,0:T(8,128)(2,1)} %bitcast.13, bf16[1,3,48,384]{3,2,1,0:T(8,128)(2,1)} %bitcast.14), kind=kLoop, calls=%fused_computation | loop fusion | flops 110592 | bytes 442368 | tf_op jit(solution)/shard_map/stack | solution.py:130
  1.0 0.0 copy-start
  1.0 0.0 copy-start.1
  1.0 5.5 %collective-permute-start = (bf16[2,3,48,384]{3,2,1,0:T(8,128)(2,1)S(1)}, bf16[2,3,48,384]{3,2,1,0:T(8,128)(2,1)S(1)}, u32[]{:S(2)}, u32[]{:S(2)}) collective-permute-start(bf16[2,3,48,384]{3,2,1,0:T(8,128)(2,1)S(1)} %pad_maximum_fusion), channel_id=1, source_target_pairs={{0,112},{16,96},{32,80},{48,64},{64,48},{80,32},{96,16},{112,0},{1... | collective-permute-start | bytes 663560 | tf_op jit(solution)/shard_map/ppermute | solution.py:132
  6.5 14.7 %all-gather = bf16[8,3,48,384]{3,2,1,0:T(8,128)(2,1)S(1)} all-gather(bf16[2,3,48,384]{3,2,1,0:T(8,128)(2,1)S(1)} %pad_maximum_fusion), channel_id=2, replica_groups=mesh['x'=4,'f'=2,'q'=4,'c'=2,'z'=8] {'x'}, dimensions={0}, use_global_device_ids=true | all-gather | bytes 1105920 | tf_op jit(solution)/shard_map/all_gather | solution.py:133
  21.2 0.0 collective-permute-done.mirror
  21.2 0.0 copy-done
  21.2 0.0 copy-done.1
  21.2 1.0 %shard_map.55 = (bf16[4,2,3,48,384]{4,3,2,1,0:T(8,128)(2,1)}, bf16[2,3,48,384]{3,2,1,0:T(8,128)(2,1)S(1)}) custom-call(bf16[2,3,48,384]{3,2,1,0:T(8,128)(2,1)S(1)} %collective-permute-done.mirror, bf16[3,48,384]{2,1,0:T(8,128)(2,1)S(1)} %copy-done, bf16[3,48,384]{2,1,0:T(8,128)(2,1)S(1)} %copy-done.1, bf16[4,2,3,48,384]{4,3,2,1,0:T(8,128)(2,1)S(1)} %bitcast.9), custom_call_target="tpu_custom_call" | custom-call | bytes 2097152 | tf_op jit(solution)/shard_map/pallas_call | solution.py:134
  22.3 5.5 %all-to-all-start = ((bf16[4,2,3,48,384]{4,3,2,1,0:T(8,128)(2,1)}), bf16[4,2,3,48,384]{4,3,2,1,0:T(8,128)(2,1)S(1)}, u32[]{:S(2)}, u32[]{:S(2)}) async-start(bf16[4,2,3,48,384]{4,3,2,1,0:T(8,128)(2,1)} %get-tuple-element.8), calls=%async_computation | async-start | bytes 1769472 | tf_op jit(solution)/shard_map/all_to_all | solution.py:137
  27.8 0.0 copy-start.2
  27.8 0.7 copy-done.2
  28.4 0.1 concatenate.3.place
  28.5 17.9 %all-gather.1 = bf16[8,3,48,384]{3,2,1,0:T(8,128)(2,1)S(1)} all-gather(bf16[2,3,48,384]{3,2,1,0:T(8,128)(2,1)S(1)} %get-tuple-element.7), channel_id=3, replica_groups=mesh['x'=4,'f'=2,'q'=4,'c'=2,'z'=8] {'q'}, dimensions={0}, use_global_device_ids=true | all-gather | bytes 1105920 | tf_op jit(solution)/shard_map/all_gather | solution.py:138
  46.5 0.0 all-to-all-done._.far
  46.5 0.6 shard_map.56.rows
  47.1 1.9 %collective-permute-start.1 = (bf16[4,2,3,48,384]{4,3,2,1,0:T(8,128)(2,1)S(1)}, bf16[4,2,3,48,384]{4,3,2,1,0:T(8,128)(2,1)S(1)}, u32[]{:S(2)}, u32[]{:S(2)}) collective-permute-start(bf16[4,2,3,48,384]{4,3,2,1,0:T(8,128)(2,1)S(1)} %shard_map.56.rows), channel_id=1, source_target_pairs={{0,8},{8,0},{1,9},{9,1},{2,10},{10,2},{3,11},{11,3},{4,12},{12,4},... | collective-permute-start | bytes 2654216 | tf_op jit(solution)/shard_map/ppermute | solution.py:140
  49.1 1.7 %shard_map.57.rest_0_ = bf16[32,56,128]{2,1,0:T(8,128)(2,1)S(1)} custom-call(s32[8]{0:T(128)S(1)} %concatenate.3.place, bf16[4,2,3,48,384]{4,3,2,1,0:T(8,128)(2,1)S(1)} %shard_map.56.rows, bf16[4,2,3,48,384]{4,3,2,1,0:T(8,128)(2,1)S(1)} %bitcast.10, bf16[4,2,3,48,384]{4,3,2,1,0:T(8,128)(2,1)S(1)} %all-to-all-done._.far), custom_call_target="tpu_custom_call" | custom-call | flops 679477248 | bytes 2097152 | tf_op jit(solution)/shard_map/pallas_call | solution.py:143
  50.8 0.7 collective-permute-done.1.rows
  51.4 1.7 %shard_map.58 = bf16[64,56,128]{2,1,0:T(8,128)(2,1)S(1)} custom-call(s32[8]{0:T(128)S(1)} %concatenate.3.place, bf16[4,2,3,48,384]{4,3,2,1,0:T(8,128)(2,1)S(1)} %collective-permute-done.1.rows, bf16[4,2,3,48,384]{4,3,2,1,0:T(8,128)(2,1)S(1)} %bitcast.11, bf16[4,2,3,48,384]{4,3,2,1,0:T(8,128)(2,1)S(1)} %all-to-all-done._.far, ...), custom_call_target="tpu_custom_call" | custom-call | flops 679477248 | bytes 2097152 | tf_op jit(solution)/shard_map/pallas_call | solution.py:143
  53.2 39.2 %all_to_all.10.pieces = bf16[64,56,128]{2,1,0:T(8,128)(2,1)S(1)} all-to-all(bf16[64,56,128]{2,1,0:T(8,128)(2,1)S(1)} %shard_map.58), channel_id=1, replica_groups=mesh['x'=4,'f'=2,'q'=4,'c'=2,'z'=8] {'q','c','z'}, dimensions={0} | all-to-all | bytes 1835008 | tf_op jit(solution)/shard_map/all_to_all | solution.py:152
  92.4 1.5 %shard_map.59 = bf16[3,48,384]{2,1,0:T(8,128)(2,1)} custom-call(s32[8]{0:T(128)S(1)} %concatenate.3.place, bf16[64,56,128]{2,1,0:T(8,128)(2,1)S(1)} %all_to_all.10.pieces), custom_call_target="tpu_custom_call" | custom-call | bytes 2097152 | tf_op jit(solution)/shard_map/pallas_call | solution.py:153
Async XLA Ops:
  1.0 20.2 %copy-start = (bf16[3,48,384]{2,1,0:T(8,128)(2,1)S(1)}, bf16[3,48,384]{2,1,0:T(8,128)(2,1)}, u32[]{:S(2)}) copy-start(bf16[3,48,384]{2,1,0:T(8,128)(2,1)} %amp.1) | copy-start | bytes 331780
  1.0 20.2 %copy-start.1 = (bf16[3,48,384]{2,1,0:T(8,128)(2,1)S(1)}, bf16[3,48,384]{2,1,0:T(8,128)(2,1)}, u32[]{:S(2)}) copy-start(bf16[3,48,384]{2,1,0:T(8,128)(2,1)} %cross.1) | copy-start | bytes 331780
  1.0 20.2 %collective-permute-start = (bf16[2,3,48,384]{3,2,1,0:T(8,128)(2,1)S(1)}, bf16[2,3,48,384]{3,2,1,0:T(8,128)(2,1)S(1)}, u32[]{:S(2)}, u32[]{:S(2)}) collective-permute-start(bf16[2,3,48,384]{3,2,1,0:T(8,128)(2,1)S(1)} %pad_maximum_fusion), channel_id=1, source_target_pairs={{0,112},{16,96},{32,80},{48,64},{64,48},{80,32},{96,16},{112,0},{1... | collective-permute-start | bytes 663560 | tf_op jit(solution)/shard_map/ppermute | solution.py:132
  22.3 24.2 %all-to-all-start = ((bf16[4,2,3,48,384]{4,3,2,1,0:T(8,128)(2,1)}), bf16[4,2,3,48,384]{4,3,2,1,0:T(8,128)(2,1)S(1)}, u32[]{:S(2)}, u32[]{:S(2)}) async-start(bf16[4,2,3,48,384]{4,3,2,1,0:T(8,128)(2,1)} %get-tuple-element.8), calls=%async_computation | async-start | bytes 1769472 | tf_op jit(solution)/shard_map/all_to_all | solution.py:137
  27.8 0.7 copy-start.2
  47.1 4.3 %collective-permute-start.1 = (bf16[4,2,3,48,384]{4,3,2,1,0:T(8,128)(2,1)S(1)}, bf16[4,2,3,48,384]{4,3,2,1,0:T(8,128)(2,1)S(1)}, u32[]{:S(2)}, u32[]{:S(2)}) collective-permute-start(bf16[4,2,3,48,384]{4,3,2,1,0:T(8,128)(2,1)S(1)} %shard_map.56.rows), channel_id=1, source_target_pairs={{0,8},{8,0},{1,9},{9,1},{2,10},{10,2},{3,11},{11,3},{4,12},{12,4},... | collective-permute-start | bytes 2654216 | tf_op jit(solution)/shard_map/ppermute | solution.py:140

commit v5 on v4

--- a/solution.py
+++ b/solution.py
@@ -24,11 +24,14 @@
 BF16 = jnp.bfloat16
 
 
-def spread_kernel(mirror, amp, cross, _, spread, left):
-    for e in range(NX):
-        spread[e] = mirror[...]
-    left[0] = amp[...]
-    left[1] = cross[...]
+def left_kernel(amp, cross, out):
+    for q in range(NQ):
+        out[q, 0] = amp[...]
+        out[q, 1] = cross[...]
+
+
+def copy_kernel(src, _, out):
+    out[...] = src[...]
 
 
 def mask_kernel(place, rows, _, out):
@@ -131,11 +134,10 @@
     n = NF * NQ
     mirror = lax.ppermute(right, ("f", "q"), [(i, n - 1 - i) for i in range(n)])
     near = lax.all_gather(right, "x")
-    spread, left = kernel(spread_kernel, [(NX,) + BLOCK, BLOCK], [VMEM] * 3 + [ANY])(
-        mirror, amplitudes, crossed, near
-    )
-    far = lax.all_to_all(spread, "x", 0, 0, tiled=True)
-    own = lax.all_gather(left, "q")
+    left = kernel(left_kernel, (NQ,) + BLOCK, [VMEM] * 2)(amplitudes, crossed)
+    own = lax.all_to_all(left, "q", 0, 0, tiled=True)
+    mirror = kernel(copy_kernel, BLOCK, [VMEM, ANY], flops=3 * 10**10)(mirror, near)
+    far = lax.all_gather(mirror, "x")
     own = kernel(mask_kernel, (NQ,) + BLOCK, [SMEM, VMEM, ANY])(place, own, far)
     other = lax.ppermute(own, "c", [(0, 1), (1, 0)])
     pieces = []

time: 94.6 us -> 90.9 us (0.961)
  blocking collectives: 71.8 us -> 69.5 us
  starting transfers between devices: 13 us -> 11.6 us
    all_gather x1, blocking collectives: 17.9 us -> 13.9 us  [local(): far = lax.all_gather(mirror, 'x')]
    all_to_all x1, blocking collectives: 39.2 us -> 41.1 us  [local(): pieces = lax.all_to_all(pieces, ('q', 'c', 'z'), 0, 0, tiled=True)]
    all_to_all x1, starting transfers between devices: 5.53 us -> 4.3 us  [local(): own = lax.all_to_all(left, 'q', 0, 0, tiled=True)]
  transfers between devices with their start and end apart: 3 -> 3, of which waited for: 1 -> 1; matrix products, arithmetic and copies ran while one was open for 0% -> 0% of each run, Pallas kernels for 2% -> 3%
where the time goes in v5:
time: 90.9 us; the launch traced here: 90.3 us
  blocking collectives  69.5 us (76%)
  starting transfers between devices  11.6 us (13%)
  Pallas kernels  6.64 us (7%)
  other arithmetic  1.02 us (1%)
    all_to_all x1, blocking collectives, local(): pieces = lax.all_to_all(pieces, ('q', 'c', 'z'), 0, 0, tiled=True)  41.1 us
    all_gather x1, blocking collectives, local(): near = lax.all_gather(right, 'x')  14.6 us
    all_gather x1, blocking collectives, local(): far = lax.all_gather(mirror, 'x')  13.9 us
    ppermute x1, starting transfers between devices, local(): mirror = lax.ppermute(right, ('f', 'q'), [(i, n - 1 - i) for i in range(n)])  5.38 us
    all_to_all x1, starting transfers between devices, local(): own = lax.all_to_all(left, 'q', 0, 0, tiled=True)  4.3 us
    pallas_call x2, Pallas kernels, local(): kernel(tile_kernel, (count,) + PACKED, [SMEM] + [VMEM] * (3 + len(pieces)...  3.44 us
    ppermute x1, starting transfers between devices, local(): other = lax.ppermute(own, 'c', [(0, 1), (1, 0)])  1.92 us
  transfers between devices with their start and end apart: 3, of which 1 were waited for; matrix products, arithmetic and copies ran while one was open for 0% of the time, Pallas kernels for 3%

profile of v5, /device:TPU:6, one launch (start us, length us, event | category | flops | bytes accessed | tf_op | source)
XLA Modules:
  0.0 90.3 jit_solution(13515190147121066222)
XLA Ops:
  0.0 0.0 copy-start
  0.0 0.0 copy-start.1
  0.0 1.0 %pad_maximum_fusion = bf16[2,3,48,384]{3,2,1,0:T(8,128)(2,1)S(1)} fusion(bf16[1,3,48,384]{3,2,1,0:T(8,128)(2,1)} %bitcast.15, bf16[1,3,48,384]{3,2,1,0:T(8,128)(2,1)} %bitcast.16), kind=kLoop, calls=%fused_computation | loop fusion | flops 110592 | bytes 442368 | tf_op jit(solution)/shard_map/stack | solution.py:133
  1.0 5.4 %collective-permute-start = (bf16[2,3,48,384]{3,2,1,0:T(8,128)(2,1)S(1)}, bf16[2,3,48,384]{3,2,1,0:T(8,128)(2,1)S(1)}, u32[]{:S(2)}, u32[]{:S(2)}) collective-permute-start(bf16[2,3,48,384]{3,2,1,0:T(8,128)(2,1)S(1)} %pad_maximum_fusion), channel_id=1, source_target_pairs={{0,112},{16,96},{32,80},{48,64},{64,48},{80,32},{96,16},{112,0},{1... | collective-permute-start | bytes 663560 | tf_op jit(solution)/shard_map/ppermute | solution.py:135
  6.4 0.0 copy-done
  6.4 0.0 copy-done.1
  6.4 1.0 %shard_map.55 = bf16[4,2,3,48,384]{4,3,2,1,0:T(8,128)(2,1)} custom-call(bf16[3,48,384]{2,1,0:T(8,128)(2,1)S(1)} %copy-done, bf16[3,48,384]{2,1,0:T(8,128)(2,1)S(1)} %copy-done.1), custom_call_target="tpu_custom_call" | custom-call | bytes 2097152 | tf_op jit(solution)/shard_map/pallas_call | solution.py:137
  7.4 4.3 %all-to-all-start = ((bf16[4,2,3,48,384]{4,3,2,1,0:T(8,128)(2,1)}), bf16[4,2,3,48,384]{4,3,2,1,0:T(8,128)(2,1)S(1)}, u32[]{:S(2)}, u32[]{:S(2)}) async-start(bf16[4,2,3,48,384]{4,3,2,1,0:T(8,128)(2,1)} %shard_map.55), calls=%async_computation | async-start | bytes 1769472 | tf_op jit(solution)/shard_map/all_to_all | solution.py:138
  11.7 0.0 copy-start.2
  11.7 0.7 copy-done.2
  12.4 0.1 concatenate.3.place
  12.5 14.6 %all-gather = bf16[8,3,48,384]{3,2,1,0:T(8,128)(2,1)S(1)} all-gather(bf16[2,3,48,384]{3,2,1,0:T(8,128)(2,1)S(1)} %pad_maximum_fusion), channel_id=2, replica_groups=mesh['x'=4,'f'=2,'q'=4,'c'=2,'z'=8] {'x'}, dimensions={0}, use_global_device_ids=true | all-gather | bytes 1105920 | tf_op jit(solution)/shard_map/all_gather | solution.py:136
  27.0 0.0 collective-permute-done.src
  27.0 13.9 %all-gather.1 = bf16[8,3,48,384]{3,2,1,0:T(8,128)(2,1)S(1)} all-gather(bf16[2,3,48,384]{3,2,1,0:T(8,128)(2,1)S(1)} %shard_map.56), channel_id=3, replica_groups=mesh['x'=4,'f'=2,'q'=4,'c'=2,'z'=8] {'x'}, dimensions={0}, use_global_device_ids=true | all-gather | bytes 1105920 | tf_op jit(solution)/shard_map/all_gather | solution.py:140
  40.9 0.0 all-to-all-done.rows
  40.9 0.6 shard_map.57.rows
  41.6 1.9 %collective-permute-start.1 = (bf16[4,2,3,48,384]{4,3,2,1,0:T(8,128)(2,1)S(1)}, bf16[4,2,3,48,384]{4,3,2,1,0:T(8,128)(2,1)S(1)}, u32[]{:S(2)}, u32[]{:S(2)}) collective-permute-start(bf16[4,2,3,48,384]{4,3,2,1,0:T(8,128)(2,1)S(1)} %shard_map.57.rows), channel_id=1, source_target_pairs={{0,8},{8,0},{1,9},{9,1},{2,10},{10,2},{3,11},{11,3},{4,12},{12,4},... | collective-permute-start | bytes 2654216 | tf_op jit(solution)/shard_map/ppermute | solution.py:142
  43.5 1.7 %shard_map.58.rest_0_ = bf16[32,56,128]{2,1,0:T(8,128)(2,1)S(1)} custom-call(s32[8]{0:T(128)S(1)} %concatenate.3.place, bf16[4,2,3,48,384]{4,3,2,1,0:T(8,128)(2,1)S(1)} %shard_map.57.rows, bf16[4,2,3,48,384]{4,3,2,1,0:T(8,128)(2,1)S(1)} %bitcast.13, bf16[4,2,3,48,384]{4,3,2,1,0:T(8,128)(2,1)S(1)} %bitcast.10), custom_call_target="tpu_custom_call" | custom-call | flops 679477248 | bytes 2097152 | tf_op jit(solution)/shard_map/pallas_call | solution.py:145
  45.2 0.7 collective-permute-done.1.rows
  45.9 1.7 %shard_map.59 = bf16[64,56,128]{2,1,0:T(8,128)(2,1)S(1)} custom-call(s32[8]{0:T(128)S(1)} %concatenate.3.place, bf16[4,2,3,48,384]{4,3,2,1,0:T(8,128)(2,1)S(1)} %collective-permute-done.1.rows, bf16[4,2,3,48,384]{4,3,2,1,0:T(8,128)(2,1)S(1)} %bitcast.14, bf16[4,2,3,48,384]{4,3,2,1,0:T(8,128)(2,1)S(1)} %bitcast.11, bf16[32,56,128]{2,1,0:T(8,128)(2,1)S(1)} %shard_map.58.rest_0_), custom_call_target="tpu_custom_call" | custom-call | flops 679477248 | bytes 2097152 | tf_op jit(solution)/shard_map/pallas_call | solution.py:145
  47.6 41.1 %all_to_all.10.pieces = bf16[64,56,128]{2,1,0:T(8,128)(2,1)S(1)} all-to-all(bf16[64,56,128]{2,1,0:T(8,128)(2,1)S(1)} %shard_map.59), channel_id=1, replica_groups=mesh['x'=4,'f'=2,'q'=4,'c'=2,'z'=8] {'q','c','z'}, dimensions={0} | all-to-all | bytes 1835008 | tf_op jit(solution)/shard_map/all_to_all | solution.py:154
  88.7 1.5 %shard_map.60 = bf16[3,48,384]{2,1,0:T(8,128)(2,1)} custom-call(s32[8]{0:T(128)S(1)} %concatenate.3.place, bf16[64,56,128]{2,1,0:T(8,128)(2,1)S(1)} %all_to_all.10.pieces), custom_call_target="tpu_custom_call" | custom-call | bytes 2097152 | tf_op jit(solution)/shard_map/pallas_call | solution.py:155
  (1 shorter events, 0.0 us)
Async XLA Ops:
  0.0 6.4 %copy-start = (bf16[3,48,384]{2,1,0:T(8,128)(2,1)S(1)}, bf16[3,48,384]{2,1,0:T(8,128)(2,1)}, u32[]{:S(2)}) copy-start(bf16[3,48,384]{2,1,0:T(8,128)(2,1)} %amp.1) | copy-start | bytes 331780
  0.0 6.4 %copy-start.1 = (bf16[3,48,384]{2,1,0:T(8,128)(2,1)S(1)}, bf16[3,48,384]{2,1,0:T(8,128)(2,1)}, u32[]{:S(2)}) copy-start(bf16[3,48,384]{2,1,0:T(8,128)(2,1)} %cross.1) | copy-start | bytes 331780
  1.0 26.0 %collective-permute-start = (bf16[2,3,48,384]{3,2,1,0:T(8,128)(2,1)S(1)}, bf16[2,3,48,384]{3,2,1,0:T(8,128)(2,1)S(1)}, u32[]{:S(2)}, u32[]{:S(2)}) collective-permute-start(bf16[2,3,48,384]{3,2,1,0:T(8,128)(2,1)S(1)} %pad_maximum_fusion), channel_id=1, source_target_pairs={{0,112},{16,96},{32,80},{48,64},{64,48},{80,32},{96,16},{112,0},{1... | collective-permute-start | bytes 663560 | tf_op jit(solution)/shard_map/ppermute | solution.py:135
  7.4 33.5 %all-to-all-start = ((bf16[4,2,3,48,384]{4,3,2,1,0:T(8,128)(2,1)}), bf16[4,2,3,48,384]{4,3,2,1,0:T(8,128)(2,1)S(1)}, u32[]{:S(2)}, u32[]{:S(2)}) async-start(bf16[4,2,3,48,384]{4,3,2,1,0:T(8,128)(2,1)} %shard_map.55), calls=%async_computation | async-start | bytes 1769472 | tf_op jit(solution)/shard_map/all_to_all | solution.py:138
  11.7 0.7 copy-start.2
  41.6 4.3 %collective-permute-start.1 = (bf16[4,2,3,48,384]{4,3,2,1,0:T(8,128)(2,1)S(1)}, bf16[4,2,3,48,384]{4,3,2,1,0:T(8,128)(2,1)S(1)}, u32[]{:S(2)}, u32[]{:S(2)}) collective-permute-start(bf16[4,2,3,48,384]{4,3,2,1,0:T(8,128)(2,1)S(1)} %shard_map.57.rows), channel_id=1, source_target_pairs={{0,8},{8,0},{1,9},{9,1},{2,10},{10,2},{3,11},{11,3},{4,12},{12,4},... | collective-permute-start | bytes 2654216 | tf_op jit(solution)/shard_map/ppermute | solution.py:142

commit v6 on v5

--- a/solution.py
+++ b/solution.py
@@ -34,7 +34,8 @@
     out[...] = src[...]
 
 
-def mask_kernel(place, rows, _, out):
+def mask_kernel(place, rows, *rest):
+    out = rest[-1]
     k = place[NH + 4] * DEPTH + lax.broadcasted_iota(jnp.int32, (1, DEPTH), 1)
     for h in range(NH):
         live = k < place[h]
@@ -44,9 +45,9 @@
                 out[q, pair, h] = jnp.where(live, block, jnp.zeros_like(block))
 
 
-def tile_kernel(place, rows, near, far, *rest):
-    before, (out, lhs, rhs) = rest[:-3], rest[-3:]
-    f, c = place[NH + 1], place[NH + 3]
+def tile_kernel(place, rows, far, *rest):
+    near, before, (out, lhs, rhs) = rest[:NX], rest[NX:-3], rest[-3:]
+    x0, f, c = place[NH], place[NH + 1], place[NH + 3]
     if before:
         for q in range(NQ):
             for z in range(NZ):
@@ -58,7 +59,7 @@
     for x in range(NX):
         for h in range(NH):
             for pair in range(2):
-                rhs[h, pair, 2 * x + f] = near[x, pair, h]
+                rhs[h, pair, 2 * lax.rem(x0 + x, NX) + f] = near[x][pair, h]
                 rhs[h, pair, 2 * x + 1 - f] = far[x, pair, h]
     totals = []
     for h in range(NH):
@@ -133,22 +134,26 @@
     right = jnp.stack([coulomb, exchange_int])
     n = NF * NQ
     mirror = lax.ppermute(right, ("f", "q"), [(i, n - 1 - i) for i in range(n)])
-    near = lax.all_gather(right, "x")
+    near = [right] + [
+        lax.ppermute(right, "x", [((i + e) % NX, i) for i in range(NX)]) for e in range(1, NX)
+    ]
     left = kernel(left_kernel, (NQ,) + BLOCK, [VMEM] * 2)(amplitudes, crossed)
     own = lax.all_to_all(left, "q", 0, 0, tiled=True)
-    mirror = kernel(copy_kernel, BLOCK, [VMEM, ANY], flops=3 * 10**10)(mirror, near)
+    mirror = kernel(copy_kernel, BLOCK, [VMEM, ANY], flops=10**10)(mirror, right)
     far = lax.all_gather(mirror, "x")
-    own = kernel(mask_kernel, (NQ,) + BLOCK, [SMEM, VMEM, ANY])(place, own, far)
+    own = kernel(mask_kernel, (NQ,) + BLOCK, [SMEM, VMEM] + [ANY] * (1 + NX))(
+        place, own, far, *near
+    )
     other = lax.ppermute(own, "c", [(0, 1), (1, 0)])
     pieces = []
     for rows, count in ((own, NQ * NZ), (other, NP * NZ)):
         pieces = kernel(
             tile_kernel,
             (count,) + PACKED,
-            [SMEM] + [VMEM] * (3 + len(pieces)),
+            [SMEM] + [VMEM] * (2 + NX + len(pieces)),
             [(NH, 2, NQ, ROWS, DEPTH), (NH, 2, NZ, ROWS, DEPTH)],
             flops=4 * NH * (NP * ROWS) ** 2 * DEPTH,
-        )(place, rows, near, far, *pieces)
+        )(place, rows, far, *near, *pieces)
         pieces = [pieces]
     pieces = pieces[0]
     pieces = lax.all_to_all(pieces, ("q", "c", "z"), 0, 0, tiled=True)

time: 90.9 us -> 89.1 us (0.980)
  blocking collectives: 69.5 us -> 58.3 us
  starting transfers between devices: 11.6 us -> 20.2 us
    all_gather x1 -> x0, blocking collectives: 14.6 us -> none  [local(): near = lax.all_gather(right, 'x')]
    ppermute x0 -> x3, starting transfers between devices: none -> 8.62 us  [local(): lax.ppermute(right, 'x', [((i + e) % NX, i) for i in range(NX)])]
    all_gather x1, blocking collectives: 13.9 us -> 18.6 us  [local(): far = lax.all_gather(mirror, 'x')]
    all_to_all x1, blocking collectives: 41.1 us -> 39.6 us  [local(): pieces = lax.all_to_all(pieces, ('q', 'c', 'z'), 0, 0, tiled=True)]
  transfers between devices with their start and end apart: 3 -> 6, of which waited for: 1 -> 1; matrix products, arithmetic and copies ran while one was open for 0% -> 0% of each run, Pallas kernels for 3% -> 3%
where the time goes in v6:
time: 89.1 us; the launch traced here: 87.7 us
  blocking collectives  58.3 us (65%)
  starting transfers between devices  20.2 us (23%)
  Pallas kernels  6.68 us (7%)
  other arithmetic  1.02 us (1%)
    all_to_all x1, blocking collectives, local(): pieces = lax.all_to_all(pieces, ('q', 'c', 'z'), 0, 0, tiled=True)  39.6 us
    all_gather x1, blocking collectives, local(): far = lax.all_gather(mirror, 'x')  18.6 us
    ppermute x3, starting transfers between devices, local(): lax.ppermute(right, 'x', [((i + e) % NX, i) for i in range(NX)])  8.62 us
    ppermute x1, starting transfers between devices, local(): mirror = lax.ppermute(right, ('f', 'q'), [(i, n - 1 - i) for i in range(n)])  5.38 us
    all_to_all x1, starting transfers between devices, local(): own = lax.all_to_all(left, 'q', 0, 0, tiled=True)  4.3 us
    pallas_call x2, Pallas kernels, local(): kernel(tile_kernel, (count,) + PACKED, [SMEM] + [VMEM] * (2 + NX + len(pi...  3.46 us
    ppermute x1, starting transfers between devices, local(): other = lax.ppermute(own, 'c', [(0, 1), (1, 0)])  1.92 us
  transfers between devices with their start and end apart: 6, of which 1 were waited for; matrix products, arithmetic and copies ran while one was open for 0% of the time, Pallas kernels for 3%

profile of v6, /device:TPU:6, one launch (start us, length us, event | category | flops | bytes accessed | tf_op | source)
XLA Modules:
  0.0 87.7 jit_solution(11416388415367347649)
XLA Ops:
  0.0 0.0 copy-start
  0.0 0.0 copy-start.1
  0.0 1.0 %pad_maximum_fusion._.rest_1_.rest_0_ = bf16[2,3,48,384]{3,2,1,0:T(8,128)(2,1)S(1)} fusion(bf16[1,3,48,384]{3,2,1,0:T(8,128)(2,1)} %bitcast.11, bf16[1,3,48,384]{3,2,1,0:T(8,128)(2,1)} %bitcast.12), kind=kLoop, calls=%fused_computation | loop fusion | flops 110592 | bytes 442368 | tf_op jit(solution)/shard_map/stack | solution.py:134
  1.0 5.4 %collective-permute-start = (bf16[2,3,48,384]{3,2,1,0:T(8,128)(2,1)S(1)}, bf16[2,3,48,384]{3,2,1,0:T(8,128)(2,1)S(1)}, u32[]{:S(2)}, u32[]{:S(2)}) collective-permute-start(bf16[2,3,48,384]{3,2,1,0:T(8,128)(2,1)S(1)} %pad_maximum_fusion._.rest_1_.rest_0_), channel_id=1, source_target_pairs={{0,112},{16,96},{32,80},{48,64},{64,48},{80,32},{96,16},{112,0},{1... | collective-permute-start | bytes 663560 | tf_op jit(solution)/shard_map/ppermute | solution.py:136
  6.4 0.0 copy-done
  6.4 0.0 copy-done.1
  6.4 1.0 %shard_map.55 = bf16[4,2,3,48,384]{4,3,2,1,0:T(8,128)(2,1)} custom-call(bf16[3,48,384]{2,1,0:T(8,128)(2,1)S(1)} %copy-done, bf16[3,48,384]{2,1,0:T(8,128)(2,1)S(1)} %copy-done.1), custom_call_target="tpu_custom_call" | custom-call | bytes 2097152 | tf_op jit(solution)/shard_map/pallas_call | solution.py:140
  7.4 4.3 %all-to-all-start = ((bf16[4,2,3,48,384]{4,3,2,1,0:T(8,128)(2,1)}), bf16[4,2,3,48,384]{4,3,2,1,0:T(8,128)(2,1)S(1)}, u32[]{:S(2)}, u32[]{:S(2)}) async-start(bf16[4,2,3,48,384]{4,3,2,1,0:T(8,128)(2,1)} %shard_map.55), calls=%async_computation | async-start | bytes 1769472 | tf_op jit(solution)/shard_map/all_to_all | solution.py:141
  11.7 3.5 %collective-permute-start.3 = (bf16[2,3,48,384]{3,2,1,0:T(8,128)(2,1)S(1)}, bf16[2,3,48,384]{3,2,1,0:T(8,128)(2,1)S(1)}, u32[]{:S(2)}, u32[]{:S(2)}) collective-permute-start(bf16[2,3,48,384]{3,2,1,0:T(8,128)(2,1)S(1)} %pad_maximum_fusion._.rest_1_.rest_0_), channel_id=1, source_target_pairs={{384,0},{0,128},{128,256},{256,384},{385,1},{1,129},{129,257},{257... | collective-permute-start | bytes 663560 | tf_op jit(solution)/shard_map/ppermute | solution.py:138
  15.3 3.2 %collective-permute-start.2 = (bf16[2,3,48,384]{3,2,1,0:T(8,128)(2,1)S(1)}, bf16[2,3,48,384]{3,2,1,0:T(8,128)(2,1)S(1)}, u32[]{:S(2)}, u32[]{:S(2)}) collective-permute-start(bf16[2,3,48,384]{3,2,1,0:T(8,128)(2,1)S(1)} %pad_maximum_fusion._.rest_1_.rest_0_), channel_id=1, source_target_pairs={{256,0},{384,128},{0,256},{128,384},{257,1},{385,129},{1,257},{129... | collective-permute-start | bytes 663560 | tf_op jit(solution)/shard_map/ppermute | solution.py:138
  18.5 1.9 %collective-permute-start.1 = (bf16[2,3,48,384]{3,2,1,0:T(8,128)(2,1)S(1)}, bf16[2,3,48,384]{3,2,1,0:T(8,128)(2,1)S(1)}, u32[]{:S(2)}, u32[]{:S(2)}) collective-permute-start(bf16[2,3,48,384]{3,2,1,0:T(8,128)(2,1)S(1)} %pad_maximum_fusion._.rest_1_.rest_0_), channel_id=1, source_target_pairs={{128,0},{256,128},{384,256},{0,384},{129,1},{257,129},{385,257},{1... | collective-permute-start | bytes 663560 | tf_op jit(solution)/shard_map/ppermute | solution.py:138
  20.4 0.0 copy-start.2
  20.4 0.6 copy-done.2
  21.1 0.1 concatenate.3.place
  21.1 0.0 collective-permute-done.src
  21.2 18.6 %all-gather = bf16[8,3,48,384]{3,2,1,0:T(8,128)(2,1)S(1)} all-gather(bf16[2,3,48,384]{3,2,1,0:T(8,128)(2,1)S(1)} %shard_map.56), channel_id=2, replica_groups=mesh['x'=4,'f'=2,'q'=4,'c'=2,'z'=8] {'x'}, dimensions={0}, use_global_device_ids=true | all-gather | bytes 1105920 | tf_op jit(solution)/shard_map/all_gather | solution.py:143
  39.8 0.0 collective-permute-done.3.rest_4_.rest_3_
  39.8 0.0 collective-permute-done.2.rest_3_.rest_2_
  39.8 0.0 collective-permute-done.1.rest_2_.rest_1_
  39.8 0.0 all-to-all-done.rows
  39.8 0.6 shard_map.57.rows
  40.5 1.9 %collective-permute-start.4 = (bf16[4,2,3,48,384]{4,3,2,1,0:T(8,128)(2,1)S(1)}, bf16[4,2,3,48,384]{4,3,2,1,0:T(8,128)(2,1)S(1)}, u32[]{:S(2)}, u32[]{:S(2)}) collective-permute-start(bf16[4,2,3,48,384]{4,3,2,1,0:T(8,128)(2,1)S(1)} %shard_map.57.rows), channel_id=1, source_target_pairs={{0,8},{8,0},{1,9},{9,1},{2,10},{10,2},{3,11},{11,3},{4,12},{12,4},... | collective-permute-start | bytes 2654216 | tf_op jit(solution)/shard_map/ppermute | solution.py:147
  42.4 1.7 %shard_map.58.rest_4_ = bf16[32,56,128]{2,1,0:T(8,128)(2,1)S(1)} custom-call(s32[8]{0:T(128)S(1)} %concatenate.3.place, bf16[4,2,3,48,384]{4,3,2,1,0:T(8,128)(2,1)S(1)} %shard_map.57.rows, bf16[4,2,3,48,384]{4,3,2,1,0:T(8,128)(2,1)S(1)} %bitcast.9, bf16[2,3,48,384]{3,2,1,0:T(8,128)(2,1)S(1)} %pad_maximum_fusion._.rest_1_.rest_0_, ...), custom_call_target="tpu_custom_call" | custom-call | flops 679477248 | bytes 2097152 | tf_op jit(solution)/shard_map/pallas_call | solution.py:150
  44.1 0.7 collective-permute-done.4.rows
  44.8 1.7 %shard_map.59 = bf16[64,56,128]{2,1,0:T(8,128)(2,1)S(1)} custom-call(s32[8]{0:T(128)S(1)} %concatenate.3.place, bf16[4,2,3,48,384]{4,3,2,1,0:T(8,128)(2,1)S(1)} %collective-permute-done.4.rows, bf16[4,2,3,48,384]{4,3,2,1,0:T(8,128)(2,1)S(1)} %bitcast.10, bf16[2,3,48,384]{3,2,1,0:T(8,128)(2,1)S(1)} %pad_maximum_fusion._.rest_1_.rest_0_, ...), custom_call_target="tpu_custom_call" | custom-call | flops 679477248 | bytes 2097152 | tf_op jit(solution)/shard_map/pallas_call | solution.py:150
  46.5 39.6 %all_to_all.10.pieces = bf16[64,56,128]{2,1,0:T(8,128)(2,1)S(1)} all-to-all(bf16[64,56,128]{2,1,0:T(8,128)(2,1)S(1)} %shard_map.59), channel_id=1, replica_groups=mesh['x'=4,'f'=2,'q'=4,'c'=2,'z'=8] {'q','c','z'}, dimensions={0} | all-to-all | bytes 1835008 | tf_op jit(solution)/shard_map/all_to_all | solution.py:159
  86.2 1.5 %shard_map.60 = bf16[3,48,384]{2,1,0:T(8,128)(2,1)} custom-call(s32[8]{0:T(128)S(1)} %concatenate.3.place, bf16[64,56,128]{2,1,0:T(8,128)(2,1)S(1)} %all_to_all.10.pieces), custom_call_target="tpu_custom_call" | custom-call | bytes 2097152 | tf_op jit(solution)/shard_map/pallas_call | solution.py:160
  (1 shorter events, 0.0 us)
Async XLA Ops:
  0.0 6.4 %copy-start = (bf16[3,48,384]{2,1,0:T(8,128)(2,1)S(1)}, bf16[3,48,384]{2,1,0:T(8,128)(2,1)}, u32[]{:S(2)}) copy-start(bf16[3,48,384]{2,1,0:T(8,128)(2,1)} %amp.1) | copy-start | bytes 331780
  0.0 6.4 %copy-start.1 = (bf16[3,48,384]{2,1,0:T(8,128)(2,1)S(1)}, bf16[3,48,384]{2,1,0:T(8,128)(2,1)}, u32[]{:S(2)}) copy-start(bf16[3,48,384]{2,1,0:T(8,128)(2,1)} %cross.1) | copy-start | bytes 331780
  1.0 20.1 %collective-permute-start = (bf16[2,3,48,384]{3,2,1,0:T(8,128)(2,1)S(1)}, bf16[2,3,48,384]{3,2,1,0:T(8,128)(2,1)S(1)}, u32[]{:S(2)}, u32[]{:S(2)}) collective-permute-start(bf16[2,3,48,384]{3,2,1,0:T(8,128)(2,1)S(1)} %pad_maximum_fusion._.rest_1_.rest_0_), channel_id=1, source_target_pairs={{0,112},{16,96},{32,80},{48,64},{64,48},{80,32},{96,16},{112,0},{1... | collective-permute-start | bytes 663560 | tf_op jit(solution)/shard_map/ppermute | solution.py:136
  7.4 32.4 %all-to-all-start = ((bf16[4,2,3,48,384]{4,3,2,1,0:T(8,128)(2,1)}), bf16[4,2,3,48,384]{4,3,2,1,0:T(8,128)(2,1)S(1)}, u32[]{:S(2)}, u32[]{:S(2)}) async-start(bf16[4,2,3,48,384]{4,3,2,1,0:T(8,128)(2,1)} %shard_map.55), calls=%async_computation | async-start | bytes 1769472 | tf_op jit(solution)/shard_map/all_to_all | solution.py:141
  11.7 28.1 %collective-permute-start.3 = (bf16[2,3,48,384]{3,2,1,0:T(8,128)(2,1)S(1)}, bf16[2,3,48,384]{3,2,1,0:T(8,128)(2,1)S(1)}, u32[]{:S(2)}, u32[]{:S(2)}) collective-permute-start(bf16[2,3,48,384]{3,2,1,0:T(8,128)(2,1)S(1)} %pad_maximum_fusion._.rest_1_.rest_0_), channel_id=1, source_target_pairs={{384,0},{0,128},{128,256},{256,384},{385,1},{1,129},{129,257},{257... | collective-permute-start | bytes 663560 | tf_op jit(solution)/shard_map/ppermute | solution.py:138
  15.3 24.5 %collective-permute-start.2 = (bf16[2,3,48,384]{3,2,1,0:T(8,128)(2,1)S(1)}, bf16[2,3,48,384]{3,2,1,0:T(8,128)(2,1)S(1)}, u32[]{:S(2)}, u32[]{:S(2)}) collective-permute-start(bf16[2,3,48,384]{3,2,1,0:T(8,128)(2,1)S(1)} %pad_maximum_fusion._.rest_1_.rest_0_), channel_id=1, source_target_pairs={{256,0},{384,128},{0,256},{128,384},{257,1},{385,129},{1,257},{129... | collective-permute-start | bytes 663560 | tf_op jit(solution)/shard_map/ppermute | solution.py:138
  18.5 21.3 %collective-permute-start.1 = (bf16[2,3,48,384]{3,2,1,0:T(8,128)(2,1)S(1)}, bf16[2,3,48,384]{3,2,1,0:T(8,128)(2,1)S(1)}, u32[]{:S(2)}, u32[]{:S(2)}) collective-permute-start(bf16[2,3,48,384]{3,2,1,0:T(8,128)(2,1)S(1)} %pad_maximum_fusion._.rest_1_.rest_0_), channel_id=1, source_target_pairs={{128,0},{256,128},{384,256},{0,384},{129,1},{257,129},{385,257},{1... | collective-permute-start | bytes 663560 | tf_op jit(solution)/shard_map/ppermute | solution.py:138
  20.4 0.7 copy-start.2
  40.5 4.3 %collective-permute-start.4 = (bf16[4,2,3,48,384]{4,3,2,1,0:T(8,128)(2,1)S(1)}, bf16[4,2,3,48,384]{4,3,2,1,0:T(8,128)(2,1)S(1)}, u32[]{:S(2)}, u32[]{:S(2)}) collective-permute-start(bf16[4,2,3,48,384]{4,3,2,1,0:T(8,128)(2,1)S(1)} %shard_map.57.rows), channel_id=1, source_target_pairs={{0,8},{8,0},{1,9},{9,1},{2,10},{10,2},{3,11},{11,3},{4,12},{12,4},... | collective-permute-start | bytes 2654216 | tf_op jit(solution)/shard_map/ppermute | solution.py:147

commit v7 on v6

v7 whole, which is shorter than its diff:
```python
import jax
import jax.numpy as jnp
from jax import lax
from jax.experimental import pallas as pl
from jax.experimental.pallas import tpu as pltpu
from jax.sharding import Mesh, PartitionSpec as P

NX, NF, NQ, NC, NZ = 4, 2, 4, 2, 8
AXES = ("x", "f", "q", "c", "z")
NH, ROWS, DEPTH = 3, 48, 384
BLOCK = (2, NH, ROWS, DEPTH)
PIECE = (NH, ROWS, DEPTH)
NP = NQ * NC
LANES = 128
LAST = 2 * ROWS
KEPT = LANES - LAST
LEFT = ROWS - KEPT
GROUP = 8
PACKED = (ROWS + GROUP, LANES)
VMEM = pl.BlockSpec(memory_space=pltpu.VMEM)
ANY = pl.BlockSpec(memory_space=pl.ANY)
SMEM = pl.BlockSpec(memory_space=pltpu.SMEM)
PARAMS = pltpu.CompilerParams(vmem_limit_bytes=32 * 2**20)
BF16 = jnp.bfloat16


def left_kernel(amp, cross, out):
    for q in range(NQ):
        out[q, 0] = amp[...]
        out[q, 1] = cross[...]


def copy_kernel(src, _, out):
    out[...] = src[...]


def mask_kernel(order, place, rows, *rest):
    out = rest[-1]
    k = place[4] * DEPTH + lax.broadcasted_iota(jnp.int32, (1, DEPTH), 1)
    for h in range(NH):
        live = k < order[h]
        for q in range(NQ):
            for pair in range(2):
                block = rows[q, pair, h]
                out[pair, h, q] = jnp.where(live, block, jnp.zeros_like(block))


def columns(place, near, far, rhs):
    x0, f = place[0], place[1]
    for x in range(NX):
        for h in range(NH):
            for pair in range(2):
                rhs[h, pair, 2 * lax.rem(x0 + x, NX) + f] = near[x][pair, h]
                rhs[h, pair, 2 * lax.rem(x0 + x, NX) + 1 - f] = far[x][pair, h]


def first_kernel(place, rows, *rest):
    near, far, (out, rhs) = rest[:NX], rest[NX : 2 * NX], rest[2 * NX :]
    columns(place, near, far, rhs)
    tile(rows, rhs, out, lambda q: q)


def second_kernel(place, rows, *rest):
    near, far = rest[:NX], rest[NX : 2 * NX]
    first, out, rhs = rest[2 * NX :]
    columns(place, near, far, rhs)
    c = place[3]
    for q in range(NQ):
        for z in range(NZ):
            out[(q * NC + c) * NZ + z] = first[q * NZ + z]
    tile(rows, rhs, out, lambda q: q * NC + 1 - c)


def tile(rows, rhs, out, at_row):
    totals = []
    for h in range(NH):
        total = None
        for pair in range(2):
            part = lax.dot_general(
                rows[pair, h].reshape(NQ * ROWS, DEPTH),
                rhs[h, pair].reshape(NZ * ROWS, DEPTH),
                (((1,), (1,)), ((), ())),
                preferred_element_type=jnp.float32,
            )
            total = part if total is None else total + part
        totals.append(total)
    fill = jnp.zeros((GROUP, LANES - ROWS // GROUP * LEFT), jnp.float32)
    for q in range(NQ):
        part = [t[q * ROWS : (q + 1) * ROWS] for t in totals]
        for z in range(NZ):
            at = z * ROWS
            main = jnp.concatenate(
                [part[0][:, at : at + ROWS], part[1][:, at : at + ROWS], part[2][:, at : at + KEPT]], axis=1
            )
            rest = part[2][:, at + KEPT : at + ROWS]
            rest = [rest[g : g + GROUP] for g in range(0, ROWS, GROUP)]
            rest = jnp.concatenate(rest + [fill], axis=1)
            out[at_row(q) * NZ + z] = jnp.concatenate([main, rest], axis=0).astype(BF16)


def sum_kernel(order, place, pieces, out):
    x, f, q, c, z = (place[i] for i in range(5))
    straight = lax.rem(z, 2) == f
    sums = []
    for s in range(NP):
        total = pieces[s * NZ].astype(jnp.float32)
        for r in range(1, NZ):
            total = total + pieces[s * NZ + r].astype(jnp.float32)
        sums.append(total)
    b = z * DEPTH + lax.broadcasted_iota(jnp.int32, (1, DEPTH), 1)
    a = (((x * NF + f) * NQ + q) * NC + c) * ROWS + lax.broadcasted_iota(jnp.int32, (ROWS, 1), 0)
    blocks = [[] for _ in range(NH)]
    for s in range(NP):
        mirrored = (NQ - 1 - s // NC) * NC + s % NC
        total = jnp.where(straight, sums[s], sums[mirrored])
        rest = [total[ROWS:, g * LEFT : (g + 1) * LEFT] for g in range(ROWS // GROUP)]
        rest = jnp.concatenate(rest, axis=0)
        blocks[0].append(total[:ROWS, :ROWS])
        blocks[1].append(total[:ROWS, ROWS:LAST])
        blocks[2].append(jnp.concatenate([total[:ROWS, LAST:], rest], axis=1))
    for h in range(NH):
        live = (a < order[h]) & (b < order[h])
        whole = jnp.concatenate(blocks[h], axis=1)
        out[h] = jnp.where(live, whole, 0.0).astype(BF16)


def kernel(body, shapes, specs, scratch=(), flops=0):
    make = lambda shape: jax.ShapeDtypeStruct(shape, BF16)
    many = isinstance(shapes, list)
    return pl.pallas_call(
        body,
        out_shape=[make(shape) for shape in shapes] if many else make(shapes),
        in_specs=specs,
        out_specs=[VMEM] * len(shapes) if many else VMEM,
        scratch_shapes=[pltpu.VMEM(shape, BF16) for shape in scratch],
        compiler_params=PARAMS,
        cost_estimate=pl.CostEstimate(flops=flops, bytes_accessed=2**21, transcendentals=0),
    )


def local(amplitudes, crossed, coulomb, exchange_int, block_order):
    place = [lax.axis_index(n) for n in AXES]
    place = jnp.stack(place).astype(jnp.int32)

    def along_x(block):
        return [block] + [
            lax.ppermute(block, "x", [((i + e) % NX, i) for i in range(NX)]) for e in range(1, NX)
        ]

    right = jnp.stack([coulomb, exchange_int])
    n = NF * NQ
    mirror = lax.ppermute(right, ("f", "q"), [(i, n - 1 - i) for i in range(n)])
    near = along_x(right)
    left = kernel(left_kernel, (NQ,) + BLOCK, [VMEM] * 2)(amplitudes, crossed)
    own = lax.all_to_all(left, "q", 0, 0, tiled=True)
    mirror = kernel(copy_kernel, BLOCK, [VMEM, ANY], flops=10**10)(mirror, right)
    far = along_x(mirror)
    own = kernel(mask_kernel, (2, NH, NQ, ROWS, DEPTH), [SMEM, SMEM, VMEM, ANY])(
        block_order, place, own, right
    )
    other = lax.ppermute(own, "c", [(0, 1), (1, 0)])
    flops = 4 * NH * (NP * ROWS) ** 2 * DEPTH
    scratch = [(NH, 2, NZ, ROWS, DEPTH)]
    specs = [SMEM] + [VMEM] * (1 + 2 * NX)
    first = kernel(first_kernel, (NQ * NZ,) + PACKED, specs, scratch, 12 * 10**9)(
        place, own, *near, *far
    )
    pieces = kernel(second_kernel, (NP * NZ,) + PACKED, specs + [VMEM], scratch, flops)(
        place, other, *near, *far, first
    )
    pieces = lax.all_to_all(pieces, ("q", "c", "z"), 0, 0, tiled=True)
    return kernel(sum_kernel, PIECE, [SMEM, SMEM, VMEM])(block_order, place, pieces)


def solution(mesh):
    grid = Mesh(mesh.devices.reshape(NX, NF, NQ, NC, NZ), AXES)
    spec = P(None, AXES[:4], "z")
    return jax.shard_map(
        local, mesh=grid, in_specs=(spec,) * 4 + (P(),), out_specs=spec, check_vma=False
    )
```

time: 89.1 us -> 85.5 us (0.960)
  blocking collectives: 58.3 us -> 40.4 us
  starting transfers between devices: 20.2 us -> 30.6 us
  waiting for transfers between devices: 0.67 us -> 5.63 us
    all_gather x1 -> x0, blocking collectives: 18.6 us -> none  [local(): far = lax.all_gather(mirror, 'x')]
    ppermute x3 -> x6, starting transfers between devices: 8.62 us -> 19 us  [along_x(): lax.ppermute(block, 'x', [((i + e) % NX, i) for i in range(NX)])]
    ppermute x3 -> x6, waiting for transfers between devices: 0.01 us -> 2.91 us  [along_x(): lax.ppermute(block, 'x', [((i + e) % NX, i) for i in range(NX)])]
    all_to_all x1, waiting for transfers between devices: 0.01 us -> 2.71 us  [local(): own = lax.all_to_all(left, 'q', 0, 0, tiled=True)]
  transfers between devices with their start and end apart: 6 -> 9, of which waited for: 1 -> 3; matrix products, arithmetic and copies ran while one was open for 0% -> 0% of each run, Pallas kernels for 3% -> 4%
where the time goes in v7:
time: 85.5 us; the launch traced here: 84.6 us
  blocking collectives  40.4 us (47%)
  starting transfers between devices  30.6 us (36%)
  Pallas kernels  6.66 us (8%)
  waiting for transfers between devices  5.63 us (7%)
  other arithmetic  1.02 us (1%)
    all_to_all x1, blocking collectives, local(): pieces = lax.all_to_all(pieces, ('q', 'c', 'z'), 0, 0, tiled=True)  40.4 us
    ppermute x6, starting transfers between devices, along_x(): lax.ppermute(block, 'x', [((i + e) % NX, i) for i in range(NX)])  19 us
    ppermute x1, starting transfers between devices, local(): mirror = lax.ppermute(right, ('f', 'q'), [(i, n - 1 - i) for i in range(n)])  5.38 us
    all_to_all x1, starting transfers between devices, local(): own = lax.all_to_all(left, 'q', 0, 0, tiled=True)  4.3 us
    ppermute x6, waiting for transfers between devices, along_x(): lax.ppermute(block, 'x', [((i + e) % NX, i) for i in range(NX)])  2.91 us
    all_to_all x1, waiting for transfers between devices, local(): own = lax.all_to_all(left, 'q', 0, 0, tiled=True)  2.71 us
    ppermute x1, starting transfers between devices, local(): other = lax.ppermute(own, 'c', [(0, 1), (1, 0)])  1.92 us
    pallas_call x1, Pallas kernels, local(): kernel(second_kernel, (NP * NZ,) + PACKED, specs + [VMEM], scratch, flops)  1.74 us
  transfers between devices with their start and end apart: 9, of which 3 were waited for; matrix products, arithmetic and copies ran while one was open for 0% of the time, Pallas kernels for 4%

profile of v7, /device:TPU:6, one launch (start us, length us, event | category | flops | bytes accessed | tf_op | source)
XLA Modules:
  0.0 84.6 jit_solution(9356312352823116179)
XLA Ops:
  0.0 0.0 copy-start
  0.0 0.0 copy-start.1
  0.0 1.0 %pad_maximum_fusion.rest_0_._ = bf16[2,3,48,384]{3,2,1,0:T(8,128)(2,1)S(1)} fusion(bf16[1,3,48,384]{3,2,1,0:T(8,128)(2,1)} %bitcast.7, bf16[1,3,48,384]{3,2,1,0:T(8,128)(2,1)} %bitcast.8), kind=kLoop, calls=%fused_computation | loop fusion | flops 110592 | bytes 442368 | tf_op jit(solution)/shard_map/stack | solution.py:150
  1.0 5.4 %collective-permute-start.4 = (bf16[2,3,48,384]{3,2,1,0:T(8,128)(2,1)S(1)}, bf16[2,3,48,384]{3,2,1,0:T(8,128)(2,1)S(1)}, u32[]{:S(2)}, u32[]{:S(2)}) collective-permute-start(bf16[2,3,48,384]{3,2,1,0:T(8,128)(2,1)S(1)} %pad_maximum_fusion.rest_0_._), channel_id=1, source_target_pairs={{0,112},{16,96},{32,80},{48,64},{64,48},{80,32},{96,16},{112,0},{1... | collective-permute-start | bytes 663560 | tf_op jit(solution)/shard_map/ppermute | solution.py:152
  6.4 0.0 copy-done
  6.4 0.0 copy-done.1
  6.4 1.0 %shard_map.55 = bf16[4,2,3,48,384]{4,3,2,1,0:T(8,128)(2,1)} custom-call(bf16[3,48,384]{2,1,0:T(8,128)(2,1)S(1)} %copy-done, bf16[3,48,384]{2,1,0:T(8,128)(2,1)S(1)} %copy-done.1), custom_call_target="tpu_custom_call" | custom-call | bytes 2097152 | tf_op jit(solution)/shard_map/pallas_call | solution.py:154
  7.4 4.3 %all-to-all-start = ((bf16[4,2,3,48,384]{4,3,2,1,0:T(8,128)(2,1)}), bf16[4,2,3,48,384]{4,3,2,1,0:T(8,128)(2,1)S(1)}, u32[]{:S(2)}, u32[]{:S(2)}) async-start(bf16[4,2,3,48,384]{4,3,2,1,0:T(8,128)(2,1)} %shard_map.55), calls=%async_computation | async-start | bytes 1769472 | tf_op jit(solution)/shard_map/all_to_all | solution.py:155
  11.7 3.5 %collective-permute-start.3 = (bf16[2,3,48,384]{3,2,1,0:T(8,128)(2,1)S(1)}, bf16[2,3,48,384]{3,2,1,0:T(8,128)(2,1)S(1)}, u32[]{:S(2)}, u32[]{:S(2)}) collective-permute-start(bf16[2,3,48,384]{3,2,1,0:T(8,128)(2,1)S(1)} %pad_maximum_fusion.rest_0_._), channel_id=1, source_target_pairs={{384,0},{0,128},{128,256},{256,384},{385,1},{1,129},{129,257},{257... | collective-permute-start | bytes 663560 | tf_op jit(solution)/shard_map/ppermute | solution.py:147
  15.3 3.2 %collective-permute-start.2 = (bf16[2,3,48,384]{3,2,1,0:T(8,128)(2,1)S(1)}, bf16[2,3,48,384]{3,2,1,0:T(8,128)(2,1)S(1)}, u32[]{:S(2)}, u32[]{:S(2)}) collective-permute-start(bf16[2,3,48,384]{3,2,1,0:T(8,128)(2,1)S(1)} %pad_maximum_fusion.rest_0_._), channel_id=1, source_target_pairs={{256,0},{384,128},{0,256},{128,384},{257,1},{385,129},{1,257},{129... | collective-permute-start | bytes 663560 | tf_op jit(solution)/shard_map/ppermute | solution.py:147
  18.4 1.9 %collective-permute-start.1 = (bf16[2,3,48,384]{3,2,1,0:T(8,128)(2,1)S(1)}, bf16[2,3,48,384]{3,2,1,0:T(8,128)(2,1)S(1)}, u32[]{:S(2)}, u32[]{:S(2)}) collective-permute-start(bf16[2,3,48,384]{3,2,1,0:T(8,128)(2,1)S(1)} %pad_maximum_fusion.rest_0_._), channel_id=1, source_target_pairs={{128,0},{256,128},{384,256},{0,384},{129,1},{257,129},{385,257},{1... | collective-permute-start | bytes 663560 | tf_op jit(solution)/shard_map/ppermute | solution.py:147
  20.4 0.0 collective-permute-done.4.src
  20.4 5.1 %collective-permute-start.7 = (bf16[2,3,48,384]{3,2,1,0:T(8,128)(2,1)S(1)}, bf16[2,3,48,384]{3,2,1,0:T(8,128)(2,1)S(1)}, u32[]{:S(2)}, u32[]{:S(2)}) collective-permute-start(bf16[2,3,48,384]{3,2,1,0:T(8,128)(2,1)S(1)} %shard_map.57.rest_4_), channel_id=1, source_target_pairs={{384,0},{0,128},{128,256},{256,384},{385,1},{1,129},{129,257},{257... | collective-permute-start | bytes 663560 | tf_op jit(solution)/shard_map/ppermute | solution.py:147
  25.6 2.9 %collective-permute-start.6 = (bf16[2,3,48,384]{3,2,1,0:T(8,128)(2,1)S(1)}, bf16[2,3,48,384]{3,2,1,0:T(8,128)(2,1)S(1)}, u32[]{:S(2)}, u32[]{:S(2)}) collective-permute-start(bf16[2,3,48,384]{3,2,1,0:T(8,128)(2,1)S(1)} %shard_map.57.rest_4_), channel_id=1, source_target_pairs={{256,0},{384,128},{0,256},{128,384},{257,1},{385,129},{1,257},{129... | collective-permute-start | bytes 663560 | tf_op jit(solution)/shard_map/ppermute | solution.py:147
  28.5 0.0 collective-permute-done.3.rest_3_
  28.5 2.3 %collective-permute-start.5 = (bf16[2,3,48,384]{3,2,1,0:T(8,128)(2,1)S(1)}, bf16[2,3,48,384]{3,2,1,0:T(8,128)(2,1)S(1)}, u32[]{:S(2)}, u32[]{:S(2)}) collective-permute-start(bf16[2,3,48,384]{3,2,1,0:T(8,128)(2,1)S(1)} %shard_map.57.rest_4_), channel_id=1, source_target_pairs={{128,0},{256,128},{384,256},{0,384},{129,1},{257,129},{385,257},{1... | collective-permute-start | bytes 663560 | tf_op jit(solution)/shard_map/ppermute | solution.py:147
  30.9 0.0 copy-start.2
  30.9 0.1 stack.32.place
  31.0 2.7 %all-to-all-done.rows = bf16[4,2,3,48,384]{4,3,2,1,0:T(8,128)(2,1)S(1)} async-done(((bf16[4,2,3,48,384]{4,3,2,1,0:T(8,128)(2,1)}), bf16[4,2,3,48,384]{4,3,2,1,0:T(8,128)(2,1)S(1)}, u32[]{:S(2)}, u32[]{:S(2)}) %all-to-all-start) | async-done | bytes 884768 | tf_op jit(solution)/shard_map/all_to_all | solution.py:155
  33.7 0.0 copy-done.2
  33.7 0.6 shard_map.56.rows
  34.3 0.0 collective-permute-done.2.rest_2_
  34.3 1.9 %collective-permute-start = (bf16[2,3,4,48,384]{4,3,2,1,0:T(8,128)(2,1)S(1)}, bf16[2,3,4,48,384]{4,3,2,1,0:T(8,128)(2,1)S(1)}, u32[]{:S(2)}, u32[]{:S(2)}) collective-permute-start(bf16[2,3,4,48,384]{4,3,2,1,0:T(8,128)(2,1)S(1)} %shard_map.56.rows), channel_id=1, source_target_pairs={{0,8},{8,0},{1,9},{9,1},{2,10},{10,2},{3,11},{11,3},{4,12},{12,4},... | collective-permute-start | bytes 2654216 | tf_op jit(solution)/shard_map/ppermute | solution.py:161
  36.3 0.0 collective-permute-done.1.rest_1_
  36.3 0.0 collective-permute-done.7.rest_7_
  36.3 0.6 collective-permute-done.6.rest_6_
  36.9 2.3 %collective-permute-done.5.rest_5_ = bf16[2,3,48,384]{3,2,1,0:T(8,128)(2,1)S(1)} collective-permute-done((bf16[2,3,48,384]{3,2,1,0:T(8,128)(2,1)S(1)}, bf16[2,3,48,384]{3,2,1,0:T(8,128)(2,1)S(1)}, u32[]{:S(2)}, u32[]{:S(2)}) %collective-permute-start.5) | collective-permute-done | bytes 221216 | tf_op jit(solution)/shard_map/ppermute | solution.py:147
  39.2 1.7 %shard_map.58.rest_8_ = bf16[32,56,128]{2,1,0:T(8,128)(2,1)S(1)} custom-call(s32[5]{0:T(128)S(1)} %stack.32.place, bf16[2,3,4,48,384]{4,3,2,1,0:T(8,128)(2,1)S(1)} %shard_map.56.rows, bf16[2,3,48,384]{3,2,1,0:T(8,128)(2,1)S(1)} %pad_maximum_fusion.rest_0_._, bf16[2,3,48,384]{3,2,1,0:T(8,128)(2,1)S(1)} %collective-permute-done.1.rest_1_, ...), custom_call_target="tpu_custom_call" | custom-call | flops 12000000000 | bytes 2097152 | tf_op jit(solution)/shard_map/pallas_call | solution.py:165
  40.9 0.0 collective-permute-done.rows
  40.9 1.7 %shard_map.59 = bf16[64,56,128]{2,1,0:T(8,128)(2,1)S(1)} custom-call(s32[5]{0:T(128)S(1)} %stack.32.place, bf16[2,3,4,48,384]{4,3,2,1,0:T(8,128)(2,1)S(1)} %collective-permute-done.rows, bf16[2,3,48,384]{3,2,1,0:T(8,128)(2,1)S(1)} %pad_maximum_fusion.rest_0_._, bf16[2,3,48,384]{3,2,1,0:T(8,128)(2,1)S(1)} %collective-permute-done.1.rest_1_, ...), custom_call_target="tpu_custom_call" | custom-call | flops 679477248 | bytes 2097152 | tf_op jit(solution)/shard_map/pallas_call | solution.py:168
  42.7 40.4 %all_to_all.10.pieces = bf16[64,56,128]{2,1,0:T(8,128)(2,1)S(1)} all-to-all(bf16[64,56,128]{2,1,0:T(8,128)(2,1)S(1)} %shard_map.59), channel_id=1, replica_groups=mesh['x'=4,'f'=2,'q'=4,'c'=2,'z'=8] {'q','c','z'}, dimensions={0} | all-to-all | bytes 1835008 | tf_op jit(solution)/shard_map/all_to_all | solution.py:171
  83.1 1.5 %shard_map.60 = bf16[3,48,384]{2,1,0:T(8,128)(2,1)} custom-call(s32[3]{0:T(128)S(1)} %copy-done.2, s32[5]{0:T(128)S(1)} %stack.32.place, bf16[64,56,128]{2,1,0:T(8,128)(2,1)S(1)} %all_to_all.10.pieces), custom_call_target="tpu_custom_call" | custom-call | bytes 2097152 | tf_op jit(solution)/shard_map/pallas_call | solution.py:172
  (1 shorter events, 0.0 us)
Async XLA Ops:
  0.0 6.4 %copy-start = (bf16[3,48,384]{2,1,0:T(8,128)(2,1)S(1)}, bf16[3,48,384]{2,1,0:T(8,128)(2,1)}, u32[]{:S(2)}) copy-start(bf16[3,48,384]{2,1,0:T(8,128)(2,1)} %amp.1) | copy-start | bytes 331780
  0.0 6.4 %copy-start.1 = (bf16[3,48,384]{2,1,0:T(8,128)(2,1)S(1)}, bf16[3,48,384]{2,1,0:T(8,128)(2,1)}, u32[]{:S(2)}) copy-start(bf16[3,48,384]{2,1,0:T(8,128)(2,1)} %cross.1) | copy-start | bytes 331780
  1.0 19.4 %collective-permute-start.4 = (bf16[2,3,48,384]{3,2,1,0:T(8,128)(2,1)S(1)}, bf16[2,3,48,384]{3,2,1,0:T(8,128)(2,1)S(1)}, u32[]{:S(2)}, u32[]{:S(2)}) collective-permute-start(bf16[2,3,48,384]{3,2,1,0:T(8,128)(2,1)S(1)} %pad_maximum_fusion.rest_0_._), channel_id=1, source_target_pairs={{0,112},{16,96},{32,80},{48,64},{64,48},{80,32},{96,16},{112,0},{1... | collective-permute-start | bytes 663560 | tf_op jit(solution)/shard_map/ppermute | solution.py:152
  7.4 26.2 %all-to-all-start = ((bf16[4,2,3,48,384]{4,3,2,1,0:T(8,128)(2,1)}), bf16[4,2,3,48,384]{4,3,2,1,0:T(8,128)(2,1)S(1)}, u32[]{:S(2)}, u32[]{:S(2)}) async-start(bf16[4,2,3,48,384]{4,3,2,1,0:T(8,128)(2,1)} %shard_map.55), calls=%async_computation | async-start | bytes 1769472 | tf_op jit(solution)/shard_map/all_to_all | solution.py:155
  11.7 16.8 %collective-permute-start.3 = (bf16[2,3,48,384]{3,2,1,0:T(8,128)(2,1)S(1)}, bf16[2,3,48,384]{3,2,1,0:T(8,128)(2,1)S(1)}, u32[]{:S(2)}, u32[]{:S(2)}) collective-permute-start(bf16[2,3,48,384]{3,2,1,0:T(8,128)(2,1)S(1)} %pad_maximum_fusion.rest_0_._), channel_id=1, source_target_pairs={{384,0},{0,128},{128,256},{256,384},{385,1},{1,129},{129,257},{257... | collective-permute-start | bytes 663560 | tf_op jit(solution)/shard_map/ppermute | solution.py:147
  15.3 19.1 %collective-permute-start.2 = (bf16[2,3,48,384]{3,2,1,0:T(8,128)(2,1)S(1)}, bf16[2,3,48,384]{3,2,1,0:T(8,128)(2,1)S(1)}, u32[]{:S(2)}, u32[]{:S(2)}) collective-permute-start(bf16[2,3,48,384]{3,2,1,0:T(8,128)(2,1)S(1)} %pad_maximum_fusion.rest_0_._), channel_id=1, source_target_pairs={{256,0},{384,128},{0,256},{128,384},{257,1},{385,129},{1,257},{129... | collective-permute-start | bytes 663560 | tf_op jit(solution)/shard_map/ppermute | solution.py:147
  18.4 17.8 %collective-permute-start.1 = (bf16[2,3,48,384]{3,2,1,0:T(8,128)(2,1)S(1)}, bf16[2,3,48,384]{3,2,1,0:T(8,128)(2,1)S(1)}, u32[]{:S(2)}, u32[]{:S(2)}) collective-permute-start(bf16[2,3,48,384]{3,2,1,0:T(8,128)(2,1)S(1)} %pad_maximum_fusion.rest_0_._), channel_id=1, source_target_pairs={{128,0},{256,128},{384,256},{0,384},{129,1},{257,129},{385,257},{1... | collective-permute-start | bytes 663560 | tf_op jit(solution)/shard_map/ppermute | solution.py:147
  20.4 15.9 %collective-permute-start.7 = (bf16[2,3,48,384]{3,2,1,0:T(8,128)(2,1)S(1)}, bf16[2,3,48,384]{3,2,1,0:T(8,128)(2,1)S(1)}, u32[]{:S(2)}, u32[]{:S(2)}) collective-permute-start(bf16[2,3,48,384]{3,2,1,0:T(8,128)(2,1)S(1)} %shard_map.57.rest_4_), channel_id=1, source_target_pairs={{384,0},{0,128},{128,256},{256,384},{385,1},{1,129},{129,257},{257... | collective-permute-start | bytes 663560 | tf_op jit(solution)/shard_map/ppermute | solution.py:147
  25.6 11.3 %collective-permute-start.6 = (bf16[2,3,48,384]{3,2,1,0:T(8,128)(2,1)S(1)}, bf16[2,3,48,384]{3,2,1,0:T(8,128)(2,1)S(1)}, u32[]{:S(2)}, u32[]{:S(2)}) collective-permute-start(bf16[2,3,48,384]{3,2,1,0:T(8,128)(2,1)S(1)} %shard_map.57.rest_4_), channel_id=1, source_target_pairs={{256,0},{384,128},{0,256},{128,384},{257,1},{385,129},{1,257},{129... | collective-permute-start | bytes 663560 | tf_op jit(solution)/shard_map/ppermute | solution.py:147
  28.5 10.7 %collective-permute-start.5 = (bf16[2,3,48,384]{3,2,1,0:T(8,128)(2,1)S(1)}, bf16[2,3,48,384]{3,2,1,0:T(8,128)(2,1)S(1)}, u32[]{:S(2)}, u32[]{:S(2)}) collective-permute-start(bf16[2,3,48,384]{3,2,1,0:T(8,128)(2,1)S(1)} %shard_map.57.rest_4_), channel_id=1, source_target_pairs={{128,0},{256,128},{384,256},{0,384},{129,1},{257,129},{385,257},{1... | collective-permute-start | bytes 663560 | tf_op jit(solution)/shard_map/ppermute | solution.py:147
  30.9 2.8 %copy-start.2 = (s32[3]{0:T(128)S(1)}, s32[3]{0:T(128)}, u32[]{:S(2)}) copy-start(s32[3]{0:T(128)} %order.3) | copy-start | bytes 40
  34.3 6.6 %collective-permute-start = (bf16[2,3,4,48,384]{4,3,2,1,0:T(8,128)(2,1)S(1)}, bf16[2,3,4,48,384]{4,3,2,1,0:T(8,128)(2,1)S(1)}, u32[]{:S(2)}, u32[]{:S(2)}) collective-permute-start(bf16[2,3,4,48,384]{4,3,2,1,0:T(8,128)(2,1)S(1)} %shard_map.56.rows), channel_id=1, source_target_pairs={{0,8},{8,0},{1,9},{9,1},{2,10},{10,2},{3,11},{11,3},{4,12},{12,4},... | collective-permute-start | bytes 2654216 | tf_op jit(solution)/shard_map/ppermute | solution.py:161

commit v8 on v7

--- a/solution.py
+++ b/solution.py
@@ -30,8 +30,8 @@
         out[q, 1] = cross[...]
 
 
-def copy_kernel(src, _, out):
-    out[...] = src[...]
+def copy_kernel(src, *rest):
+    rest[-1][...] = src[...]
 
 
 def mask_kernel(order, place, rows, *rest):
@@ -45,45 +45,32 @@
                 out[pair, h, q] = jnp.where(live, block, jnp.zeros_like(block))
 
 
-def columns(place, near, far, rhs):
-    x0, f = place[0], place[1]
+def tile_kernel(place, own, other, *rest):
+    near, far, (out, rhs) = rest[:NX], rest[NX : 2 * NX], rest[2 * NX :]
+    x0, f, c = place[0], place[1], place[3]
     for x in range(NX):
         for h in range(NH):
             for pair in range(2):
                 rhs[h, pair, 2 * lax.rem(x0 + x, NX) + f] = near[x][pair, h]
                 rhs[h, pair, 2 * lax.rem(x0 + x, NX) + 1 - f] = far[x][pair, h]
+    for side, rows in enumerate((own, other)):
+        core = lax.rem(c + side, NC)
+        totals = []
+        for h in range(NH):
+            total = None
+            for pair in range(2):
+                part = lax.dot_general(
+                    rows[pair, h].reshape(NQ * ROWS, DEPTH),
+                    rhs[h, pair].reshape(NZ * ROWS, DEPTH),
+                    (((1,), (1,)), ((), ())),
+                    preferred_element_type=jnp.float32,
+                )
+                total = part if total is None else total + part
+            totals.append(total)
+        pack(totals, out, core)
 
 
-def first_kernel(place, rows, *rest):
-    near, far, (out, rhs) = rest[:NX], rest[NX : 2 * NX], rest[2 * NX :]
-    columns(place, near, far, rhs)
-    tile(rows, rhs, out, lambda q: q)
-
-
-def second_kernel(place, rows, *rest):
-    near, far = rest[:NX], rest[NX : 2 * NX]
-    first, out, rhs = rest[2 * NX :]
-    columns(place, near, far, rhs)
-    c = place[3]
-    for q in range(NQ):
-        for z in range(NZ):
-            out[(q * NC + c) * NZ + z] = first[q * NZ + z]
-    tile(rows, rhs, out, lambda q: q * NC + 1 - c)
-
-
-def tile(rows, rhs, out, at_row):
-    totals = []
-    for h in range(NH):
-        total = None
-        for pair in range(2):
-            part = lax.dot_general(
-                rows[pair, h].reshape(NQ * ROWS, DEPTH),
-                rhs[h, pair].reshape(NZ * ROWS, DEPTH),
-                (((1,), (1,)), ((), ())),
-                preferred_element_type=jnp.float32,
-            )
-            total = part if total is None else total + part
-        totals.append(total)
+def pack(totals, out, core):
     fill = jnp.zeros((GROUP, LANES - ROWS // GROUP * LEFT), jnp.float32)
     for q in range(NQ):
         part = [t[q * ROWS : (q + 1) * ROWS] for t in totals]
@@ -95,7 +82,7 @@
             rest = part[2][:, at + KEPT : at + ROWS]
             rest = [rest[g : g + GROUP] for g in range(0, ROWS, GROUP)]
             rest = jnp.concatenate(rest + [fill], axis=1)
-            out[at_row(q) * NZ + z] = jnp.concatenate([main, rest], axis=0).astype(BF16)
+            out[(q * NC + core) * NZ + z] = jnp.concatenate([main, rest], axis=0).astype(BF16)
 
 
 def sum_kernel(order, place, pieces, out):
@@ -160,14 +147,16 @@
     )
     other = lax.ppermute(own, "c", [(0, 1), (1, 0)])
     flops = 4 * NH * (NP * ROWS) ** 2 * DEPTH
-    scratch = [(NH, 2, NZ, ROWS, DEPTH)]
-    specs = [SMEM] + [VMEM] * (1 + 2 * NX)
-    first = kernel(first_kernel, (NQ * NZ,) + PACKED, specs, scratch, 12 * 10**9)(
-        place, own, *near, *far
+    last = kernel(copy_kernel, BLOCK, [VMEM] + [ANY] * 5, flops=12 * 10**9)(
+        far[3], far[1], far[2], *near[1:]
     )
-    pieces = kernel(second_kernel, (NP * NZ,) + PACKED, specs + [VMEM], scratch, flops)(
-        place, other, *near, *far, first
-    )
+    pieces = kernel(
+        tile_kernel,
+        (NP * NZ,) + PACKED,
+        [SMEM] + [VMEM] * (2 + 2 * NX),
+        [(NH, 2, NZ, ROWS, DEPTH)],
+        flops,
+    )(place, own, other, *near, *far[:3], last)
     pieces = lax.all_to_all(pieces, ("q", "c", "z"), 0, 0, tiled=True)
     return kernel(sum_kernel, PIECE, [SMEM, SMEM, VMEM])(block_order, place, pieces)
 

time: 85.5 us -> 84.4 us (0.987)
  Pallas kernels: 6.66 us -> 5.67 us
    pallas_call x2, Pallas kernels: 3.45 us -> 2.45 us  [the longest x1 2.43 us: local(): kernel(tile_kernel, (NP * NZ,) + PACKED, [SMEM] + [VMEM] * (2 + 2 * NX),...]
  transfers between devices with their start and end apart: 9 -> 9, of which waited for: 3 -> 3; matrix products, arithmetic and copies ran while one was open for 0% -> 0% of each run, Pallas kernels for 4% -> 2%
where the time goes in v8:
time: 84.4 us; the launch traced here: 83.6 us
  blocking collectives  40.4 us (48%)
  starting transfers between devices  30.6 us (36%)
  Pallas kernels  5.67 us (7%)
  waiting for transfers between devices  5.63 us (7%)
  other arithmetic  1.02 us (1%)
    all_to_all x1, blocking collectives, local(): pieces = lax.all_to_all(pieces, ('q', 'c', 'z'), 0, 0, tiled=True)  40.4 us
    ppermute x6, starting transfers between devices, along_x(): lax.ppermute(block, 'x', [((i + e) % NX, i) for i in range(NX)])  19 us
    ppermute x1, starting transfers between devices, local(): mirror = lax.ppermute(right, ('f', 'q'), [(i, n - 1 - i) for i in range(n)])  5.38 us
    all_to_all x1, starting transfers between devices, local(): own = lax.all_to_all(left, 'q', 0, 0, tiled=True)  4.3 us
    ppermute x6, waiting for transfers between devices, along_x(): lax.ppermute(block, 'x', [((i + e) % NX, i) for i in range(NX)])  2.91 us
    all_to_all x1, waiting for transfers between devices, local(): own = lax.all_to_all(left, 'q', 0, 0, tiled=True)  2.71 us
    pallas_call x1, Pallas kernels, local(): kernel(tile_kernel, (NP * NZ,) + PACKED, [SMEM] + [VMEM] * (2 + 2 * NX),...  2.43 us
    ppermute x1, starting transfers between devices, local(): other = lax.ppermute(own, 'c', [(0, 1), (1, 0)])  1.92 us
  transfers between devices with their start and end apart: 9, of which 3 were waited for; matrix products, arithmetic and copies ran while one was open for 0% of the time, Pallas kernels for 2%

profile of v8, /device:TPU:6, one launch (start us, length us, event | category | flops | bytes accessed | tf_op | source)
XLA Modules:
  0.0 83.6 jit_solution(4935731402521437223)
XLA Ops:
  0.0 0.0 copy-start
  0.0 0.0 copy-start.1
  0.0 1.0 %pad_maximum_fusion.rest_0_ = bf16[2,3,48,384]{3,2,1,0:T(8,128)(2,1)S(1)} fusion(bf16[1,3,48,384]{3,2,1,0:T(8,128)(2,1)} %bitcast.7, bf16[1,3,48,384]{3,2,1,0:T(8,128)(2,1)} %bitcast.8), kind=kLoop, calls=%fused_computation | loop fusion | flops 110592 | bytes 442368 | tf_op jit(solution)/shard_map/stack | solution.py:137
  1.0 5.4 %collective-permute-start.4 = (bf16[2,3,48,384]{3,2,1,0:T(8,128)(2,1)S(1)}, bf16[2,3,48,384]{3,2,1,0:T(8,128)(2,1)S(1)}, u32[]{:S(2)}, u32[]{:S(2)}) collective-permute-start(bf16[2,3,48,384]{3,2,1,0:T(8,128)(2,1)S(1)} %pad_maximum_fusion.rest_0_), channel_id=1, source_target_pairs={{0,112},{16,96},{32,80},{48,64},{64,48},{80,32},{96,16},{112,0},{1... | collective-permute-start | bytes 663560 | tf_op jit(solution)/shard_map/ppermute | solution.py:139
  6.4 0.0 copy-done
  6.4 0.0 copy-done.1
  6.4 1.0 %shard_map.55 = bf16[4,2,3,48,384]{4,3,2,1,0:T(8,128)(2,1)} custom-call(bf16[3,48,384]{2,1,0:T(8,128)(2,1)S(1)} %copy-done, bf16[3,48,384]{2,1,0:T(8,128)(2,1)S(1)} %copy-done.1), custom_call_target="tpu_custom_call" | custom-call | bytes 2097152 | tf_op jit(solution)/shard_map/pallas_call | solution.py:141
  7.4 4.3 %all-to-all-start = ((bf16[4,2,3,48,384]{4,3,2,1,0:T(8,128)(2,1)}), bf16[4,2,3,48,384]{4,3,2,1,0:T(8,128)(2,1)S(1)}, u32[]{:S(2)}, u32[]{:S(2)}) async-start(bf16[4,2,3,48,384]{4,3,2,1,0:T(8,128)(2,1)} %shard_map.55), calls=%async_computation | async-start | bytes 1769472 | tf_op jit(solution)/shard_map/all_to_all | solution.py:142
  11.7 3.5 %collective-permute-start.3 = (bf16[2,3,48,384]{3,2,1,0:T(8,128)(2,1)S(1)}, bf16[2,3,48,384]{3,2,1,0:T(8,128)(2,1)S(1)}, u32[]{:S(2)}, u32[]{:S(2)}) collective-permute-start(bf16[2,3,48,384]{3,2,1,0:T(8,128)(2,1)S(1)} %pad_maximum_fusion.rest_0_), channel_id=1, source_target_pairs={{384,0},{0,128},{128,256},{256,384},{385,1},{1,129},{129,257},{257... | collective-permute-start | bytes 663560 | tf_op jit(solution)/shard_map/ppermute | solution.py:134
  15.3 3.2 %collective-permute-start.2 = (bf16[2,3,48,384]{3,2,1,0:T(8,128)(2,1)S(1)}, bf16[2,3,48,384]{3,2,1,0:T(8,128)(2,1)S(1)}, u32[]{:S(2)}, u32[]{:S(2)}) collective-permute-start(bf16[2,3,48,384]{3,2,1,0:T(8,128)(2,1)S(1)} %pad_maximum_fusion.rest_0_), channel_id=1, source_target_pairs={{256,0},{384,128},{0,256},{128,384},{257,1},{385,129},{1,257},{129... | collective-permute-start | bytes 663560 | tf_op jit(solution)/shard_map/ppermute | solution.py:134
  18.4 1.9 %collective-permute-start.1 = (bf16[2,3,48,384]{3,2,1,0:T(8,128)(2,1)S(1)}, bf16[2,3,48,384]{3,2,1,0:T(8,128)(2,1)S(1)}, u32[]{:S(2)}, u32[]{:S(2)}) collective-permute-start(bf16[2,3,48,384]{3,2,1,0:T(8,128)(2,1)S(1)} %pad_maximum_fusion.rest_0_), channel_id=1, source_target_pairs={{128,0},{256,128},{384,256},{0,384},{129,1},{257,129},{385,257},{1... | collective-permute-start | bytes 663560 | tf_op jit(solution)/shard_map/ppermute | solution.py:134
  20.4 0.0 collective-permute-done.4.src
  20.4 5.1 %collective-permute-start.7 = (bf16[2,3,48,384]{3,2,1,0:T(8,128)(2,1)S(1)}, bf16[2,3,48,384]{3,2,1,0:T(8,128)(2,1)S(1)}, u32[]{:S(2)}, u32[]{:S(2)}) collective-permute-start(bf16[2,3,48,384]{3,2,1,0:T(8,128)(2,1)S(1)} %shard_map.57.rest_4_), channel_id=1, source_target_pairs={{384,0},{0,128},{128,256},{256,384},{385,1},{1,129},{129,257},{257... | collective-permute-start | bytes 663560 | tf_op jit(solution)/shard_map/ppermute | solution.py:134
  25.6 2.9 %collective-permute-start.6 = (bf16[2,3,48,384]{3,2,1,0:T(8,128)(2,1)S(1)}, bf16[2,3,48,384]{3,2,1,0:T(8,128)(2,1)S(1)}, u32[]{:S(2)}, u32[]{:S(2)}) collective-permute-start(bf16[2,3,48,384]{3,2,1,0:T(8,128)(2,1)S(1)} %shard_map.57.rest_4_), channel_id=1, source_target_pairs={{256,0},{384,128},{0,256},{128,384},{257,1},{385,129},{1,257},{129... | collective-permute-start | bytes 663560 | tf_op jit(solution)/shard_map/ppermute | solution.py:134
  28.5 0.0 collective-permute-done.3.rest_4_.rest_3_
  28.5 2.3 %collective-permute-start.5 = (bf16[2,3,48,384]{3,2,1,0:T(8,128)(2,1)S(1)}, bf16[2,3,48,384]{3,2,1,0:T(8,128)(2,1)S(1)}, u32[]{:S(2)}, u32[]{:S(2)}) collective-permute-start(bf16[2,3,48,384]{3,2,1,0:T(8,128)(2,1)S(1)} %shard_map.57.rest_4_), channel_id=1, source_target_pairs={{128,0},{256,128},{384,256},{0,384},{129,1},{257,129},{385,257},{1... | collective-permute-start | bytes 663560 | tf_op jit(solution)/shard_map/ppermute | solution.py:134
  30.9 0.0 copy-start.2
  30.9 0.1 stack.32.place
  31.0 2.7 %all-to-all-done.rows = bf16[4,2,3,48,384]{4,3,2,1,0:T(8,128)(2,1)S(1)} async-done(((bf16[4,2,3,48,384]{4,3,2,1,0:T(8,128)(2,1)}), bf16[4,2,3,48,384]{4,3,2,1,0:T(8,128)(2,1)S(1)}, u32[]{:S(2)}, u32[]{:S(2)}) %all-to-all-start) | async-done | bytes 884768 | tf_op jit(solution)/shard_map/all_to_all | solution.py:142
  33.7 0.0 copy-done.2
  33.7 0.6 shard_map.56.own
  34.3 0.0 collective-permute-done.2.rest_3_.rest_2_
  34.3 1.9 %collective-permute-start = (bf16[2,3,4,48,384]{4,3,2,1,0:T(8,128)(2,1)S(1)}, bf16[2,3,4,48,384]{4,3,2,1,0:T(8,128)(2,1)S(1)}, u32[]{:S(2)}, u32[]{:S(2)}) collective-permute-start(bf16[2,3,4,48,384]{4,3,2,1,0:T(8,128)(2,1)S(1)} %shard_map.56.own), channel_id=1, source_target_pairs={{0,8},{8,0},{1,9},{9,1},{2,10},{10,2},{3,11},{11,3},{4,12},{12,4},... | collective-permute-start | bytes 2654216 | tf_op jit(solution)/shard_map/ppermute | solution.py:148
  36.3 0.0 collective-permute-done.1.rest_2_.rest_1_
  36.3 0.0 collective-permute-done.7.src
  36.3 0.6 collective-permute-done.6.rest_1_.rest_6_
  36.9 2.3 %collective-permute-done.5.rest_0_.rest_5_ = bf16[2,3,48,384]{3,2,1,0:T(8,128)(2,1)S(1)} collective-permute-done((bf16[2,3,48,384]{3,2,1,0:T(8,128)(2,1)S(1)}, bf16[2,3,48,384]{3,2,1,0:T(8,128)(2,1)S(1)}, u32[]{:S(2)}, u32[]{:S(2)}) %collective-permute-start.5) | collective-permute-done | bytes 221216 | tf_op jit(solution)/shard_map/ppermute | solution.py:134
  39.2 0.0 collective-permute-done.other
  39.2 2.4 %shard_map.59 = bf16[64,56,128]{2,1,0:T(8,128)(2,1)S(1)} custom-call(s32[5]{0:T(128)S(1)} %stack.32.place, bf16[2,3,4,48,384]{4,3,2,1,0:T(8,128)(2,1)S(1)} %shard_map.56.own, bf16[2,3,4,48,384]{4,3,2,1,0:T(8,128)(2,1)S(1)} %collective-permute-done.other, bf16[2,3,48,384]{3,2,1,0:T(8,128)(2,1)S(1)} %pad_maximum_fusion.rest_0_, ...), custom_call_target="tpu_custom_call" | custom-call | flops 679477248 | bytes 2097152 | tf_op jit(solution)/shard_map/pallas_call | solution.py:153
  41.7 40.4 %all_to_all.10.pieces = bf16[64,56,128]{2,1,0:T(8,128)(2,1)S(1)} all-to-all(bf16[64,56,128]{2,1,0:T(8,128)(2,1)S(1)} %shard_map.59), channel_id=1, replica_groups=mesh['x'=4,'f'=2,'q'=4,'c'=2,'z'=8] {'q','c','z'}, dimensions={0} | all-to-all | bytes 1835008 | tf_op jit(solution)/shard_map/all_to_all | solution.py:160
  82.0 1.5 %shard_map.60 = bf16[3,48,384]{2,1,0:T(8,128)(2,1)} custom-call(s32[3]{0:T(128)S(1)} %copy-done.2, s32[5]{0:T(128)S(1)} %stack.32.place, bf16[64,56,128]{2,1,0:T(8,128)(2,1)S(1)} %all_to_all.10.pieces), custom_call_target="tpu_custom_call" | custom-call | bytes 2097152 | tf_op jit(solution)/shard_map/pallas_call | solution.py:161
  (2 shorter events, 0.0 us)
Async XLA Ops:
  0.0 6.4 %copy-start = (bf16[3,48,384]{2,1,0:T(8,128)(2,1)S(1)}, bf16[3,48,384]{2,1,0:T(8,128)(2,1)}, u32[]{:S(2)}) copy-start(bf16[3,48,384]{2,1,0:T(8,128)(2,1)} %amp.1) | copy-start | bytes 331780
  0.0 6.4 %copy-start.1 = (bf16[3,48,384]{2,1,0:T(8,128)(2,1)S(1)}, bf16[3,48,384]{2,1,0:T(8,128)(2,1)}, u32[]{:S(2)}) copy-start(bf16[3,48,384]{2,1,0:T(8,128)(2,1)} %cross.1) | copy-start | bytes 331780
  1.0 19.4 %collective-permute-start.4 = (bf16[2,3,48,384]{3,2,1,0:T(8,128)(2,1)S(1)}, bf16[2,3,48,384]{3,2,1,0:T(8,128)(2,1)S(1)}, u32[]{:S(2)}, u32[]{:S(2)}) collective-permute-start(bf16[2,3,48,384]{3,2,1,0:T(8,128)(2,1)S(1)} %pad_maximum_fusion.rest_0_), channel_id=1, source_target_pairs={{0,112},{16,96},{32,80},{48,64},{64,48},{80,32},{96,16},{112,0},{1... | collective-permute-start | bytes 663560 | tf_op jit(solution)/shard_map/ppermute | solution.py:139
  7.4 26.2 %all-to-all-start = ((bf16[4,2,3,48,384]{4,3,2,1,0:T(8,128)(2,1)}), bf16[4,2,3,48,384]{4,3,2,1,0:T(8,128)(2,1)S(1)}, u32[]{:S(2)}, u32[]{:S(2)}) async-start(bf16[4,2,3,48,384]{4,3,2,1,0:T(8,128)(2,1)} %shard_map.55), calls=%async_computation | async-start | bytes 1769472 | tf_op jit(solution)/shard_map/all_to_all | solution.py:142
  11.7 16.8 %collective-permute-start.3 = (bf16[2,3,48,384]{3,2,1,0:T(8,128)(2,1)S(1)}, bf16[2,3,48,384]{3,2,1,0:T(8,128)(2,1)S(1)}, u32[]{:S(2)}, u32[]{:S(2)}) collective-permute-start(bf16[2,3,48,384]{3,2,1,0:T(8,128)(2,1)S(1)} %pad_maximum_fusion.rest_0_), channel_id=1, source_target_pairs={{384,0},{0,128},{128,256},{256,384},{385,1},{1,129},{129,257},{257... | collective-permute-start | bytes 663560 | tf_op jit(solution)/shard_map/ppermute | solution.py:134
  15.3 19.1 %collective-permute-start.2 = (bf16[2,3,48,384]{3,2,1,0:T(8,128)(2,1)S(1)}, bf16[2,3,48,384]{3,2,1,0:T(8,128)(2,1)S(1)}, u32[]{:S(2)}, u32[]{:S(2)}) collective-permute-start(bf16[2,3,48,384]{3,2,1,0:T(8,128)(2,1)S(1)} %pad_maximum_fusion.rest_0_), channel_id=1, source_target_pairs={{256,0},{384,128},{0,256},{128,384},{257,1},{385,129},{1,257},{129... | collective-permute-start | bytes 663560 | tf_op jit(solution)/shard_map/ppermute | solution.py:134
  18.4 17.8 %collective-permute-start.1 = (bf16[2,3,48,384]{3,2,1,0:T(8,128)(2,1)S(1)}, bf16[2,3,48,384]{3,2,1,0:T(8,128)(2,1)S(1)}, u32[]{:S(2)}, u32[]{:S(2)}) collective-permute-start(bf16[2,3,48,384]{3,2,1,0:T(8,128)(2,1)S(1)} %pad_maximum_fusion.rest_0_), channel_id=1, source_target_pairs={{128,0},{256,128},{384,256},{0,384},{129,1},{257,129},{385,257},{1... | collective-permute-start | bytes 663560 | tf_op jit(solution)/shard_map/ppermute | solution.py:134
  20.4 15.9 %collective-permute-start.7 = (bf16[2,3,48,384]{3,2,1,0:T(8,128)(2,1)S(1)}, bf16[2,3,48,384]{3,2,1,0:T(8,128)(2,1)S(1)}, u32[]{:S(2)}, u32[]{:S(2)}) collective-permute-start(bf16[2,3,48,384]{3,2,1,0:T(8,128)(2,1)S(1)} %shard_map.57.rest_4_), channel_id=1, source_target_pairs={{384,0},{0,128},{128,256},{256,384},{385,1},{1,129},{129,257},{257... | collective-permute-start | bytes 663560 | tf_op jit(solution)/shard_map/ppermute | solution.py:134
  25.6 11.3 %collective-permute-start.6 = (bf16[2,3,48,384]{3,2,1,0:T(8,128)(2,1)S(1)}, bf16[2,3,48,384]{3,2,1,0:T(8,128)(2,1)S(1)}, u32[]{:S(2)}, u32[]{:S(2)}) collective-permute-start(bf16[2,3,48,384]{3,2,1,0:T(8,128)(2,1)S(1)} %shard_map.57.rest_4_), channel_id=1, source_target_pairs={{256,0},{384,128},{0,256},{128,384},{257,1},{385,129},{1,257},{129... | collective-permute-start | bytes 663560 | tf_op jit(solution)/shard_map/ppermute | solution.py:134
  28.5 10.7 %collective-permute-start.5 = (bf16[2,3,48,384]{3,2,1,0:T(8,128)(2,1)S(1)}, bf16[2,3,48,384]{3,2,1,0:T(8,128)(2,1)S(1)}, u32[]{:S(2)}, u32[]{:S(2)}) collective-permute-start(bf16[2,3,48,384]{3,2,1,0:T(8,128)(2,1)S(1)} %shard_map.57.rest_4_), channel_id=1, source_target_pairs={{128,0},{256,128},{384,256},{0,384},{129,1},{257,129},{385,257},{1... | collective-permute-start | bytes 663560 | tf_op jit(solution)/shard_map/ppermute | solution.py:134
  30.9 2.8 %copy-start.2 = (s32[3]{0:T(128)S(1)}, s32[3]{0:T(128)}, u32[]{:S(2)}) copy-start(s32[3]{0:T(128)} %order.3) | copy-start | bytes 40
  34.3 4.9 %collective-permute-start = (bf16[2,3,4,48,384]{4,3,2,1,0:T(8,128)(2,1)S(1)}, bf16[2,3,4,48,384]{4,3,2,1,0:T(8,128)(2,1)S(1)}, u32[]{:S(2)}, u32[]{:S(2)}) collective-permute-start(bf16[2,3,4,48,384]{4,3,2,1,0:T(8,128)(2,1)S(1)} %shard_map.56.own), channel_id=1, source_target_pairs={{0,8},{8,0},{1,9},{9,1},{2,10},{10,2},{3,11},{11,3},{4,12},{12,4},... | collective-permute-start | bytes 2654216 | tf_op jit(solution)/shard_map/ppermute | solution.py:148
